TPU v7x, 32 devices: a whole 2x2x4 slice. The times are simulated.
32 devices in a mesh: prefix: 4 (over y, x), cand: 8 (over z, core).
Axes of the slice: x: 2, y: 2, z: 4, core: 2. Of those that a mesh axis runs over, the one named last changes fastest.
Arguments:
- query: bfloat16 [2048, 8192], P('cand', 'prefix'), may hold values from -100 to 100
- grad_out: bfloat16 [2048, 8192], P('cand', 'prefix'), may hold values from -24 to 24
- continuation_key: bfloat16 [2048, 1024], P('cand', 'prefix'), may hold values from -8 to 8
- continuation_value: bfloat16 [2048, 1024], P('cand', 'prefix'), may hold values from -6 to 6
- prompt_key: bfloat16 [768, 1024], P(('prefix', 'cand')), may hold values from -4 to 4
- shared_prompt_value: bfloat16 [768, 1024], P(('prefix', 'cand')), may hold values from -6 to 6
- assign: int32 [32], replicated, may hold values from 0 to 7, as said below
- lengths: int32 [32], replicated, may hold values from 1 to 64, as said below
- offsets: int32 [32], replicated, may hold values from 384 to 768
Outputs:
- query_grad: bfloat16 [2048, 8192], P('cand', 'prefix')
- cont_key_grad: bfloat16 [2048, 1024], P('cand', 'prefix')
- cont_value_grad: bfloat16 [2048, 1024], P('cand', 'prefix')
- prompt_key_grad: bfloat16 [768, 1024], P(('prefix', 'cand'))
- prompt_value_grad: bfloat16 [768, 1024], P(('prefix', 'cand'))
Inputs may be any that keep to these rules, and one draw needn't show every extreme that they name: `assign`: each index of cand is named by exactly 4 candidates. The lengths of the candidates on one index of cand sum to at most 256; on some index they sum to exactly 256, each of its candidates having length 64.
All inputs are finite; a program needn't handle non-finite values.
Results may differ from a plain program's by a relative error of at most 0.015.
Values may be sent and summed in bfloat16 or wider, within the bound.
No kernel may reach another device: no remote copies, remote signals or barrier semaphores. Data moves between devices by JAX's collectives and lax.ppermute only.
A program may use at most 64 MiB of HBM per device.

v0:
```python
import math

import jax
import jax.numpy as jnp
from jax import lax
from jax.sharding import PartitionSpec as P

HEAD_WIDTH = 128


MASKED_SCORE = -1e30


def slot_layout(assign, lengths, offsets, device, slot_count):
    cand_count = assign.shape[0]
    cand_order = jnp.arange(cand_count, dtype=jnp.int32)
    earlier_same = (assign[:, None] == assign[None, :]) & (
        cand_order[None, :] < cand_order[:, None]
    )
    starts = jnp.sum(jnp.where(earlier_same, lengths[None, :], 0), axis=1)
    slot_index = jnp.arange(slot_count, dtype=jnp.int32)
    slot_match = (
        (assign[:, None] == device)
        & (slot_index[None, :] >= starts[:, None])
        & (slot_index[None, :] < (starts + lengths)[:, None])
    )
    row_valid = jnp.any(slot_match, axis=0)
    row_segment = jnp.sum(jnp.where(slot_match, cand_order[:, None], 0), axis=0)
    offset_row = jnp.sum(jnp.where(slot_match, offsets[:, None], 0), axis=0)
    return (row_valid, row_segment, offset_row)


def attend(
    queries,
    grad_rows,
    joined_keys,
    joined_values,
    key_segment,
    key_position,
    row_valid,
    row_segment,
    offset_row,
):
    row_count = queries.shape[0]
    head_count = joined_keys.shape[1]
    head_size = joined_keys.shape[2]
    key_count = joined_keys.shape[0]
    block_size = math.gcd(key_count, 256)
    block_count = key_count // block_size
    score_scale = 1.0 / math.sqrt(head_size)
    query_heads = queries.reshape(row_count, head_count, -1, head_size)
    grad_heads = grad_rows.reshape(query_heads.shape)
    slot_index = jnp.arange(row_count, dtype=jnp.int32)
    stacked = (
        joined_keys.reshape(block_count, block_size, head_count, head_size),
        joined_values.reshape(block_count, block_size, head_count, head_size),
        key_segment.reshape(block_count, block_size),
        key_position.reshape(block_count, block_size),
    )

    def scores(block_items):
        key_block, value_block, block_segment, block_position = block_items
        prompt_ok = (block_segment[None, :] == -1) & (block_position[None, :] < offset_row[:, None])
        cont_ok = (block_segment[None, :] == row_segment[:, None]) & (
            block_position[None, :] <= slot_index[:, None]
        )
        visible_mask = (row_valid[:, None] & (prompt_ok | cont_ok))[None, None]
        raw_scores = (
            jnp.einsum("rhgd,jhd->hgrj", query_heads, key_block, preferred_element_type=jnp.float32)
            * score_scale
        )
        return (raw_scores, visible_mask)

    def normaliser(state_pair, block_items):
        running_max, summed = state_pair
        raw_scores, visible_mask = scores(block_items)
        fresh_max = jnp.maximum(
            running_max, jnp.max(jnp.where(visible_mask, raw_scores, MASKED_SCORE), axis=3)
        )
        summed = summed * jnp.exp(running_max - fresh_max) + jnp.sum(
            jnp.where(visible_mask, jnp.exp(raw_scores - fresh_max[..., None]), 0.0), axis=3
        )
        return ((fresh_max, summed), None)

    stat_shape = (head_count, query_heads.shape[2], row_count)
    start_pair = (
        jnp.full(stat_shape, MASKED_SCORE, jnp.float32),
        jnp.zeros(stat_shape, jnp.float32),
    )
    (running_max, summed), _ = lax.scan(normaliser, start_pair, stacked)
    lse = running_max + jnp.log(jnp.where(row_valid[None, None, :], summed, 1.0))

    def weighting(raw_scores, visible_mask):
        return jnp.where(visible_mask, jnp.exp(raw_scores - lse[..., None]), 0.0)

    def forward(attended, block_items):
        raw_scores, visible_mask = scores(block_items)
        probs_bf = weighting(raw_scores, visible_mask).astype(jnp.bfloat16)
        return (
            attended
            + jnp.einsum(
                "hgrj,jhd->rhgd", probs_bf, block_items[1], preferred_element_type=jnp.float32
            ),
            None,
        )

    attended, _ = lax.scan(forward, jnp.zeros(query_heads.shape, jnp.float32), stacked)
    row_delta = jnp.transpose(jnp.sum(grad_heads.astype(jnp.float32) * attended, axis=3), (1, 2, 0))

    def backward(grad_query, block_items):
        raw_scores, visible_mask = scores(block_items)
        weights = weighting(raw_scores, visible_mask)
        probs_bf = weights.astype(jnp.bfloat16)
        prob_grad = jnp.einsum(
            "rhgd,jhd->hgrj", grad_heads, block_items[1], preferred_element_type=jnp.float32
        )
        score_grad = (weights * (prob_grad - row_delta[..., None])).astype(jnp.bfloat16)
        value_sum = jnp.einsum(
            "hgrj,rhgd->jhd", probs_bf, grad_heads, preferred_element_type=jnp.float32
        )
        key_sum = (
            jnp.einsum(
                "hgrj,rhgd->jhd", score_grad, query_heads, preferred_element_type=jnp.float32
            )
            * score_scale
        )
        grad_query = grad_query + jnp.einsum(
            "hgrj,jhd->rhgd", score_grad, block_items[0], preferred_element_type=jnp.float32
        )
        return (grad_query, (key_sum, value_sum))

    grad_query, (key_sums, value_sums) = lax.scan(
        backward, jnp.zeros(query_heads.shape, jnp.float32), stacked
    )
    return (
        grad_query * score_scale,
        key_sums.reshape(key_count, head_count, head_size),
        value_sums.reshape(key_count, head_count, head_size),
    )


def per_device(
    query,
    grad_out,
    continuation_key,
    continuation_value,
    prompt_key,
    shared_prompt_value,
    assign,
    lengths,
    offsets,
):
    row_count = query.shape[0]
    prefix_count = lax.axis_size("prefix")
    owned_rows = prompt_key.shape[0]
    local_width = prompt_key.shape[1] // prefix_count
    local_heads = local_width // HEAD_WIDTH
    block_keys, block_values = (
        lax.all_gather(prompt_key, "cand", axis=0, tiled=True),
        lax.all_gather(shared_prompt_value, "cand", axis=0, tiled=True),
    )
    block_rows = block_keys.shape[0]
    split_keys, split_values = (
        lax.all_to_all(
            block_keys.reshape(block_rows, prefix_count, local_width),
            "prefix",
            split_axis=1,
            concat_axis=0,
            tiled=True,
        ),
        lax.all_to_all(
            block_values.reshape(block_rows, prefix_count, local_width),
            "prefix",
            split_axis=1,
            concat_axis=0,
            tiled=True,
        ),
    )
    full_keys = split_keys.reshape(-1, local_width)
    full_values = split_values.reshape(-1, local_width)
    prompt_len = full_keys.shape[0]
    device = lax.axis_index("cand")
    row_valid, row_segment, offset_row = slot_layout(assign, lengths, offsets, device, row_count)
    joined_keys = jnp.concatenate(
        [
            full_keys.reshape(prompt_len, local_heads, HEAD_WIDTH),
            continuation_key.reshape(row_count, local_heads, HEAD_WIDTH),
        ],
        axis=0,
    )
    joined_values = jnp.concatenate(
        [
            full_values.reshape(prompt_len, local_heads, HEAD_WIDTH),
            continuation_value.reshape(row_count, local_heads, HEAD_WIDTH),
        ],
        axis=0,
    )
    key_segment = jnp.concatenate(
        [jnp.full((prompt_len,), -1, jnp.int32), jnp.where(row_valid, row_segment, -2)]
    )
    key_position = jnp.concatenate(
        [jnp.arange(prompt_len, dtype=jnp.int32), jnp.arange(row_count, dtype=jnp.int32)]
    )
    grad_query, key_sums, value_sums = attend(
        query,
        grad_out,
        joined_keys,
        joined_values,
        key_segment,
        key_position,
        row_valid,
        row_segment,
        offset_row,
    )
    query_grad = grad_query.reshape(row_count, -1).astype(jnp.bfloat16)
    cont_key_grad = key_sums[prompt_len:].reshape(row_count, local_width).astype(jnp.bfloat16)
    cont_value_grad = value_sums[prompt_len:].reshape(row_count, local_width).astype(jnp.bfloat16)
    prompt_keys_part = key_sums[:prompt_len].reshape(prompt_len, local_width).astype(jnp.bfloat16)
    prompt_values_part = (
        value_sums[:prompt_len].reshape(prompt_len, local_width).astype(jnp.bfloat16)
    )
    block_rows = prompt_len // prefix_count
    arrived_keys, arrived_values = (
        lax.all_to_all(
            prompt_keys_part.reshape(prefix_count, block_rows, 1, local_width),
            "prefix",
            split_axis=0,
            concat_axis=2,
            tiled=True,
        ),
        lax.all_to_all(
            prompt_values_part.reshape(prefix_count, block_rows, 1, local_width),
            "prefix",
            split_axis=0,
            concat_axis=2,
            tiled=True,
        ),
    )
    summed_keys, summed_values = (
        lax.psum_scatter(arrived_keys, "cand", scatter_dimension=1, tiled=True).astype(jnp.float32),
        lax.psum_scatter(arrived_values, "cand", scatter_dimension=1, tiled=True).astype(
            jnp.float32
        ),
    )
    prompt_key_grad = summed_keys.reshape(owned_rows, -1).astype(jnp.bfloat16)
    prompt_value_grad = summed_values.reshape(owned_rows, -1).astype(jnp.bfloat16)
    return (query_grad, cont_key_grad, cont_value_grad, prompt_key_grad, prompt_value_grad)


def solution(mesh):
    in_specs = (
        P("cand", "prefix"),
        P("cand", "prefix"),
        P("cand", "prefix"),
        P("cand", "prefix"),
        P(("prefix", "cand"), None),
        P(("prefix", "cand"), None),
        P(),
        P(),
        P(),
    )
    out_specs = (
        P("cand", "prefix"),
        P("cand", "prefix"),
        P("cand", "prefix"),
        P(("prefix", "cand"), None),
        P(("prefix", "cand"), None),
    )
    return jax.shard_map(
        per_device, mesh=mesh, in_specs=in_specs, out_specs=out_specs, check_vma=False
    )
```

profile of v0, /device:TPU:0, one launch (start us, length us, event | category | flops | bytes accessed | tf_op | source)
XLA Modules:
  0.0 244.1 jit_solution(4063014974033678660)
XLA Ops:
  7.2 16.6 %all_gather.6 = bf16[192,1024]{1,0:T(8,128)(2,1)S(1)} all-gather(bf16[24,1024]{1,0:T(8,128)(2,1)} %param.19), channel_id=1, replica_groups=mesh['prefix'=4,'cand'=8] {'cand'}, dimensions={0}, use_global_device_ids=true | all-gather | bytes 442368 | tf_op jit(solution)/shard_map/all_gather | solution.py:159
  24.5 3.7 %all-to-all-start = ((bf16[192,4,256]{2,0,1:T(8,128)(2,1)}), bf16[192,4,256]{2,0,1:T(8,128)(2,1)S(1)}, u32[]{:S(2)}, u32[]{:S(2)}) async-start(bf16[192,4,256]{2,0,1:T(8,128)(2,1)} %bitcast.194), calls=%async_computation | async-start | bytes 786432 | tf_op jit(solution)/shard_map/all_to_all | solution.py:164
  28.2 14.6 %all_gather.7 = bf16[192,1024]{1,0:T(8,128)(2,1)S(1)} all-gather(bf16[24,1024]{1,0:T(8,128)(2,1)} %param.20), channel_id=1, replica_groups=mesh['prefix'=4,'cand'=8] {'cand'}, dimensions={0}, use_global_device_ids=true | all-gather | bytes 442368 | tf_op jit(solution)/shard_map/all_gather | solution.py:160
  47.3 4.2 %all-to-all-start.1 = ((bf16[192,4,256]{2,0,1:T(8,128)(2,1)}), bf16[192,4,256]{2,0,1:T(8,128)(2,1)}, u32[]{:S(2)}, u32[]{:S(2)}) async-start(bf16[192,4,256]{2,0,1:T(8,128)(2,1)} %bitcast.193), calls=%async_computation.1 | async-start | bytes 786432 | tf_op jit(solution)/shard_map/all_to_all | solution.py:171
  57.0 2.3 copy.102
  61.7 1.7 pad_maximum_fusion
  67.9 21.8 %while.39 = (s32[]{:T(128)}, f32[2,8,256]{2,1,0:T(8,128)S(1)}, f32[2,8,256]{2,1,0:T(8,128)}, pred[256]{0:T(512)(128)(4,1)}, s32[4,256]{1,0:T(4,128)}, /*index=5*...) while((s32[]{:T(128)}, f32[2,8,256]{2,1,0:T(8,128)S(1)}, ...), condition=%wide.region_7.8_spmd.clone, body=%wide.region_4.7_spmd.clone.sunk | while | flops 276254976 | bytes 10118092 | solution.py:90
  70.2 1.7 fusion.104
  75.7 1.7 fusion.104
  81.1 1.7 fusion.104
  86.6 1.7 fusion.104
  90.5 25.4 %while.40 = (s32[]{:T(128)}, f32[256,2,8,128]{0,3,2,1:T(8,128)}, bf16[4,256,2,128]{3,1,0,2:T(8,128)(2,1)}, pred[256]{0:T(512)(128)(4,1)}, s32[4,256]{1,0:T(4,128...) while((s32[]{:T(128)}, f32[256,2,8,128]{0,3,2,1:T(8,128)}, ...), condition=%wide.region_9.10_spmd.clone, body=%wide.region_8.9_spmd.clone.sunk | while | flops 542572800 | bytes 5663126 | solution.py:107
  92.8 3.5 %bitcast_add_fusion.4 = f32[256,2,8,128]{0,3,2,1:T(8,128)} fusion(f32[256,2,8,128]{0,3,2,1:T(8,128)} %get-tuple-element.862, bf16[256,2,8,128]{3,0,2,1:T(8,128)(2,1)S(1)} %get-tuple-element.883, f32[2,8,256]{2,1,0:T(8,128)S(1)} %get-tuple-element.884, pred[256,256]{0,1:T(8,128)(4,1)S(1)} %fusion.110, pred[]{:T(512)S(6)} %compare.11, ...), kind=kOutput, calls=%fused_computation.27.clone.1 | convolution fusion | flops 542113792 | bytes 5588480 | tf_op jit(solution)/shard_map/while/body/eval_jaxpr/hgrj,jhd->rhgd/dot_general | solution.py:101
  98.5 4.3 %bitcast_add_fusion.4 = f32[256,2,8,128]{0,3,2,1:T(8,128)} fusion(f32[256,2,8,128]{0,3,2,1:T(8,128)} %get-tuple-element.862, bf16[256,2,8,128]{3,0,2,1:T(8,128)(2,1)S(1)} %get-tuple-element.883, f32[2,8,256]{2,1,0:T(8,128)S(1)} %get-tuple-element.884, pred[256,256]{0,1:T(8,128)(4,1)S(1)} %fusion.110, pred[]{:T(512)S(6)} %compare.11, ...), kind=kOutput, calls=%fused_computation.27.clone.1 | convolution fusion | flops 542113792 | bytes 5588480 | tf_op jit(solution)/shard_map/while/body/eval_jaxpr/hgrj,jhd->rhgd/dot_general | solution.py:101
  105.1 4.3 %bitcast_add_fusion.4 = f32[256,2,8,128]{0,3,2,1:T(8,128)} fusion(f32[256,2,8,128]{0,3,2,1:T(8,128)} %get-tuple-element.862, bf16[256,2,8,128]{3,0,2,1:T(8,128)(2,1)S(1)} %get-tuple-element.883, f32[2,8,256]{2,1,0:T(8,128)S(1)} %get-tuple-element.884, pred[256,256]{0,1:T(8,128)(4,1)S(1)} %fusion.110, pred[]{:T(512)S(6)} %compare.11, ...), kind=kOutput, calls=%fused_computation.27.clone.1 | convolution fusion | flops 542113792 | bytes 5588480 | tf_op jit(solution)/shard_map/while/body/eval_jaxpr/hgrj,jhd->rhgd/dot_general | solution.py:101
  111.6 4.3 %bitcast_add_fusion.4 = f32[256,2,8,128]{0,3,2,1:T(8,128)} fusion(f32[256,2,8,128]{0,3,2,1:T(8,128)} %get-tuple-element.862, bf16[256,2,8,128]{3,0,2,1:T(8,128)(2,1)S(1)} %get-tuple-element.883, f32[2,8,256]{2,1,0:T(8,128)S(1)} %get-tuple-element.884, pred[256,256]{0,1:T(8,128)(4,1)S(1)} %fusion.110, pred[]{:T(512)S(6)} %compare.11, ...), kind=kOutput, calls=%fused_computation.27.clone.1 | convolution fusion | flops 542113792 | bytes 5588480 | tf_op jit(solution)/shard_map/while/body/eval_jaxpr/hgrj,jhd->rhgd/dot_general | solution.py:101
  115.9 2.1 multiply_reduce_fusion
  118.1 41.7 %while.41 = (s32[]{:T(128)}, f32[256,2,8,128]{0,3,2,1:T(8,128)S(1)}, bf16[4,256,2,128]{3,1,2,0:T(8,128)(2,1)}, bf16[4,256,2,128]{3,1,2,0:T(8,128)(2,1)}, bf16[4,...) while((s32[]{:T(128)}, ...), condition=%wide.region_12.13_spmd.clone, body=%wide.region_11.12_spmd.clone.sunk | while | flops 1354236160 | bytes 41018452 | solution.py:132
  120.4 1.6 fusion.121
  123.1 2.5 %fusion.123 = bf16[2,8,256,256]{2,3,1,0:T(8,128)(2,1)S(1)} fusion(f32[2,256,256,8]{2,1,3,0:T(8,128)S(1)} %fusion.121, bf16[256,2,8,128]{3,0,2,1:T(8,128)(2,1)S(1)} %copy-done.1, f32[2,8,256]{2,1,0:T(8,128)S(1)} %get-tuple-element.935, f32[2,8,256]{2,1,0:T(8,128)S(1)} %get-tuple-element.932, pred[256,256]{0,1:T(8,128)(4,1)S(1)} %fusion.122, ...), kind=kOutput, calls=%fused_computation.44.clone.1 | convolution fusion | flops 274726912 | bytes 7569412 | tf_op jit(solution)/shard_map/while/body/eval_jaxpr/rhgd,jhd->hgrj/dot_general | solution.py:114
  126.4 2.0 bitcast_add_fusion.5
  133.5 2.5 %fusion.123 = bf16[2,8,256,256]{2,3,1,0:T(8,128)(2,1)S(1)} fusion(f32[2,256,256,8]{2,1,3,0:T(8,128)S(1)} %fusion.121, bf16[256,2,8,128]{3,0,2,1:T(8,128)(2,1)S(1)} %copy-done.1, f32[2,8,256]{2,1,0:T(8,128)S(1)} %get-tuple-element.935, f32[2,8,256]{2,1,0:T(8,128)S(1)} %get-tuple-element.932, pred[256,256]{0,1:T(8,128)(4,1)S(1)} %fusion.122, ...), kind=kOutput, calls=%fused_computation.44.clone.1 | convolution fusion | flops 274726912 | bytes 7569412 | tf_op jit(solution)/shard_map/while/body/eval_jaxpr/rhgd,jhd->hgrj/dot_general | solution.py:114
  136.9 2.0 bitcast_add_fusion.5
  141.3 1.6 fusion.121
  144.0 2.5 %fusion.123 = bf16[2,8,256,256]{2,3,1,0:T(8,128)(2,1)S(1)} fusion(f32[2,256,256,8]{2,1,3,0:T(8,128)S(1)} %fusion.121, bf16[256,2,8,128]{3,0,2,1:T(8,128)(2,1)S(1)} %copy-done.1, f32[2,8,256]{2,1,0:T(8,128)S(1)} %get-tuple-element.935, f32[2,8,256]{2,1,0:T(8,128)S(1)} %get-tuple-element.932, pred[256,256]{0,1:T(8,128)(4,1)S(1)} %fusion.122, ...), kind=kOutput, calls=%fused_computation.44.clone.1 | convolution fusion | flops 274726912 | bytes 7569412 | tf_op jit(solution)/shard_map/while/body/eval_jaxpr/rhgd,jhd->hgrj/dot_general | solution.py:114
  147.3 2.0 bitcast_add_fusion.5
  154.4 2.5 %fusion.123 = bf16[2,8,256,256]{2,3,1,0:T(8,128)(2,1)S(1)} fusion(f32[2,256,256,8]{2,1,3,0:T(8,128)S(1)} %fusion.121, bf16[256,2,8,128]{3,0,2,1:T(8,128)(2,1)S(1)} %copy-done.1, f32[2,8,256]{2,1,0:T(8,128)S(1)} %get-tuple-element.935, f32[2,8,256]{2,1,0:T(8,128)S(1)} %get-tuple-element.932, pred[256,256]{0,1:T(8,128)(4,1)S(1)} %fusion.122, ...), kind=kOutput, calls=%fused_computation.44.clone.1 | convolution fusion | flops 274726912 | bytes 7569412 | tf_op jit(solution)/shard_map/while/body/eval_jaxpr/rhgd,jhd->hgrj/dot_general | solution.py:114
  157.7 2.0 bitcast_add_fusion.5
  161.5 11.6 %all_to_all.66 = bf16[4,192,1,256]{3,1,2,0:T(8,128)(2,1)S(1)} all-to-all(bf16[4,192,1,256]{3,1,2,0:T(8,128)(2,1)S(1)} %bitcast.265), channel_id=1, replica_groups=mesh['prefix'=4,'cand'=8] {'prefix'}, dimensions={0} | all-to-all | bytes 786432 | tf_op jit(solution)/shard_map/all_to_all | solution.py:231
  175.0 8.8 %all_to_all.67 = bf16[4,192,1,256]{3,1,2,0:T(8,128)(2,1)S(1)} all-to-all(bf16[4,192,1,256]{3,1,2,0:T(8,128)(2,1)S(1)} %bitcast.268), channel_id=1, replica_groups=mesh['prefix'=4,'cand'=8] {'prefix'}, dimensions={0} | all-to-all | bytes 786432 | tf_op jit(solution)/shard_map/all_to_all | solution.py:224
  189.3 15.4 %reduce-scatter.9.cloned.1.call-done = bf16[24,1024]{1,0:T(8,128)(2,1)} async-done(((bf16[192,1024]{1,0:T(8,128)(2,1)}), bf16[24,1024]{1,0:T(8,128)(2,1)}) %reduce-scatter.9.cloned.1.call-update) | async-done | bytes 49168
  206.1 29.7 %reduce-scatter.7.cloned.1.call-done = bf16[24,1024]{1,0:T(8,128)(2,1)} async-done(((bf16[192,1024]{1,0:T(8,128)(2,1)}), bf16[24,1024]{1,0:T(8,128)(2,1)}) %reduce-scatter.7.cloned.1.call-update) | async-done | bytes 49168
  (191 shorter events, 73.8 us)
Async XLA Ops:
  7.2 45.6 %copy-start.12 = (bf16[256,256]{1,0:T(8,128)(2,1)S(1)}, bf16[256,256]{1,0:T(8,128)(2,1)}, u32[]{:S(2)}) copy-start(bf16[256,256]{1,0:T(8,128)(2,1)} %param.17) | copy-start | bytes 393220
  7.2 46.3 %copy-start.13 = (bf16[256,256]{1,0:T(8,128)(2,1)S(1)}, bf16[256,256]{1,0:T(8,128)(2,1)}, u32[]{:S(2)}) copy-start(bf16[256,256]{1,0:T(8,128)(2,1)} %param.18) | copy-start | bytes 393220
  24.5 22.8 %all-to-all-start = ((bf16[192,4,256]{2,0,1:T(8,128)(2,1)}), bf16[192,4,256]{2,0,1:T(8,128)(2,1)S(1)}, u32[]{:S(2)}, u32[]{:S(2)}) async-start(bf16[192,4,256]{2,0,1:T(8,128)(2,1)} %bitcast.194), calls=%async_computation | async-start | bytes 786432 | tf_op jit(solution)/shard_map/all_to_all | solution.py:164
  46.0 7.5 %copy-start.11 = (pred[256]{0:T(512)(128)(4,1)}, pred[256]{0:T(512)(128)(4,1)S(1)}, u32[]{:S(2)}) copy-start(pred[256]{0:T(512)(128)(4,1)S(1)} %fusion.69) | copy-start | bytes 772
  47.3 6.2 %copy-start.10 = (s32[256]{0:T(256)}, s32[256]{0:T(256)S(1)}, u32[]{:S(2)}) copy-start(s32[256]{0:T(256)S(1)} %get-tuple-element.896) | copy-start | bytes 3076
  47.3 17.1 %all-to-all-start.1 = ((bf16[192,4,256]{2,0,1:T(8,128)(2,1)}), bf16[192,4,256]{2,0,1:T(8,128)(2,1)}, u32[]{:S(2)}, u32[]{:S(2)}) async-start(bf16[192,4,256]{2,0,1:T(8,128)(2,1)} %bitcast.193), calls=%async_computation.1 | async-start | bytes 786432 | tf_op jit(solution)/shard_map/all_to_all | solution.py:171
  51.5 153.2 %reduce-scatter.9.cloned.1.call-start = ((), (), s32[]{:S(2)}) async-start(), calls=%async_computation.7 | async-start | bytes 442368
  55.7 3.6 %copy-start = (bf16[256,2048]{0,1:T(8,128)(2,1)}, bf16[256,2048]{0,1:T(8,128)(2,1)S(1)}, u32[]{:S(2)}) copy-start(bf16[256,2048]{0,1:T(8,128)(2,1)S(1)} %copy.107) | copy-start | bytes 3145732
  70.2 2.6 %copy-start.2 = (f32[2,8,256]{2,1,0:T(8,128)S(1)}, f32[2,8,256]{2,1,0:T(8,128)}, u32[]{:S(2)}) copy-start(f32[2,8,256]{2,1,0:T(8,128)} %get-tuple-element.826) | copy-start | bytes 49156 | tf_op jit(solution)/shard_map/while
  75.6 2.6 %copy-start.2 = (f32[2,8,256]{2,1,0:T(8,128)S(1)}, f32[2,8,256]{2,1,0:T(8,128)}, u32[]{:S(2)}) copy-start(f32[2,8,256]{2,1,0:T(8,128)} %get-tuple-element.826) | copy-start | bytes 49156 | tf_op jit(solution)/shard_map/while
  81.1 2.6 %copy-start.2 = (f32[2,8,256]{2,1,0:T(8,128)S(1)}, f32[2,8,256]{2,1,0:T(8,128)}, u32[]{:S(2)}) copy-start(f32[2,8,256]{2,1,0:T(8,128)} %get-tuple-element.826) | copy-start | bytes 49156 | tf_op jit(solution)/shard_map/while
  86.5 2.6 %copy-start.2 = (f32[2,8,256]{2,1,0:T(8,128)S(1)}, f32[2,8,256]{2,1,0:T(8,128)}, u32[]{:S(2)}) copy-start(f32[2,8,256]{2,1,0:T(8,128)} %get-tuple-element.826) | copy-start | bytes 49156 | tf_op jit(solution)/shard_map/while
  118.1 4.0 %copy-start.1 = (bf16[256,2,8,128]{3,0,2,1:T(8,128)(2,1)S(1)}, bf16[256,2,8,128]{3,0,2,1:T(8,128)(2,1)}, u32[]{:S(2)}) copy-start(bf16[256,2,8,128]{3,0,2,1:T(8,128)(2,1)} %get-tuple-element.934) | copy-start | bytes 3145732 | tf_op jit(solution)/shard_map/while
  118.1 4.0 %copy-start.4 = (bf16[4,256,2,128]{3,1,2,0:T(8,128)(2,1)S(1)}, bf16[4,256,2,128]{3,1,2,0:T(8,128)(2,1)}, u32[]{:S(2)}) copy-start(bf16[4,256,2,128]{3,1,2,0:T(8,128)(2,1)} %get-tuple-element.907) | copy-start | bytes 1572868 | tf_op jit(solution)/shard_map/while
  123.1 3.3 %copy-start.5 = (bf16[4,256,2,128]{3,1,2,0:T(8,128)(2,1)}, bf16[4,256,2,128]{3,1,2,0:T(8,128)(2,1)S(1)}, u32[]{:S(2)}) copy-start(bf16[4,256,2,128]{3,1,2,0:T(8,128)(2,1)S(1)} %fusion.125) | copy-start | bytes 1572868 | tf_op jit(solution)/shard_map/while
  123.1 2.5 %copy-start.6 = (bf16[4,256,2,128]{3,1,2,0:T(8,128)(2,1)S(1)}, bf16[4,256,2,128]{3,1,2,0:T(8,128)(2,1)}, u32[]{:S(2)}) copy-start(bf16[4,256,2,128]{3,1,2,0:T(8,128)(2,1)} %get-tuple-element.906) | copy-start | bytes 1572868 | tf_op jit(solution)/shard_map/while
  128.5 4.0 %copy-start.1 = (bf16[256,2,8,128]{3,0,2,1:T(8,128)(2,1)S(1)}, bf16[256,2,8,128]{3,0,2,1:T(8,128)(2,1)}, u32[]{:S(2)}) copy-start(bf16[256,2,8,128]{3,0,2,1:T(8,128)(2,1)} %get-tuple-element.934) | copy-start | bytes 3145732 | tf_op jit(solution)/shard_map/while
  128.5 4.0 %copy-start.4 = (bf16[4,256,2,128]{3,1,2,0:T(8,128)(2,1)S(1)}, bf16[4,256,2,128]{3,1,2,0:T(8,128)(2,1)}, u32[]{:S(2)}) copy-start(bf16[4,256,2,128]{3,1,2,0:T(8,128)(2,1)} %get-tuple-element.907) | copy-start | bytes 1572868 | tf_op jit(solution)/shard_map/while
  133.5 3.3 %copy-start.5 = (bf16[4,256,2,128]{3,1,2,0:T(8,128)(2,1)}, bf16[4,256,2,128]{3,1,2,0:T(8,128)(2,1)S(1)}, u32[]{:S(2)}) copy-start(bf16[4,256,2,128]{3,1,2,0:T(8,128)(2,1)S(1)} %fusion.125) | copy-start | bytes 1572868 | tf_op jit(solution)/shard_map/while
  133.5 2.5 %copy-start.6 = (bf16[4,256,2,128]{3,1,2,0:T(8,128)(2,1)S(1)}, bf16[4,256,2,128]{3,1,2,0:T(8,128)(2,1)}, u32[]{:S(2)}) copy-start(bf16[4,256,2,128]{3,1,2,0:T(8,128)(2,1)} %get-tuple-element.906) | copy-start | bytes 1572868 | tf_op jit(solution)/shard_map/while
  138.9 4.0 %copy-start.1 = (bf16[256,2,8,128]{3,0,2,1:T(8,128)(2,1)S(1)}, bf16[256,2,8,128]{3,0,2,1:T(8,128)(2,1)}, u32[]{:S(2)}) copy-start(bf16[256,2,8,128]{3,0,2,1:T(8,128)(2,1)} %get-tuple-element.934) | copy-start | bytes 3145732 | tf_op jit(solution)/shard_map/while
  138.9 4.0 %copy-start.4 = (bf16[4,256,2,128]{3,1,2,0:T(8,128)(2,1)S(1)}, bf16[4,256,2,128]{3,1,2,0:T(8,128)(2,1)}, u32[]{:S(2)}) copy-start(bf16[4,256,2,128]{3,1,2,0:T(8,128)(2,1)} %get-tuple-element.907) | copy-start | bytes 1572868 | tf_op jit(solution)/shard_map/while
  144.0 3.3 %copy-start.5 = (bf16[4,256,2,128]{3,1,2,0:T(8,128)(2,1)}, bf16[4,256,2,128]{3,1,2,0:T(8,128)(2,1)S(1)}, u32[]{:S(2)}) copy-start(bf16[4,256,2,128]{3,1,2,0:T(8,128)(2,1)S(1)} %fusion.125) | copy-start | bytes 1572868 | tf_op jit(solution)/shard_map/while
  144.0 2.5 %copy-start.6 = (bf16[4,256,2,128]{3,1,2,0:T(8,128)(2,1)S(1)}, bf16[4,256,2,128]{3,1,2,0:T(8,128)(2,1)}, u32[]{:S(2)}) copy-start(bf16[4,256,2,128]{3,1,2,0:T(8,128)(2,1)} %get-tuple-element.906) | copy-start | bytes 1572868 | tf_op jit(solution)/shard_map/while
  147.3 2.0 copy-start.7
  149.4 4.0 %copy-start.1 = (bf16[256,2,8,128]{3,0,2,1:T(8,128)(2,1)S(1)}, bf16[256,2,8,128]{3,0,2,1:T(8,128)(2,1)}, u32[]{:S(2)}) copy-start(bf16[256,2,8,128]{3,0,2,1:T(8,128)(2,1)} %get-tuple-element.934) | copy-start | bytes 3145732 | tf_op jit(solution)/shard_map/while
  149.4 4.0 %copy-start.4 = (bf16[4,256,2,128]{3,1,2,0:T(8,128)(2,1)S(1)}, bf16[4,256,2,128]{3,1,2,0:T(8,128)(2,1)}, u32[]{:S(2)}) copy-start(bf16[4,256,2,128]{3,1,2,0:T(8,128)(2,1)} %get-tuple-element.907) | copy-start | bytes 1572868 | tf_op jit(solution)/shard_map/while
  154.4 3.3 %copy-start.5 = (bf16[4,256,2,128]{3,1,2,0:T(8,128)(2,1)}, bf16[4,256,2,128]{3,1,2,0:T(8,128)(2,1)S(1)}, u32[]{:S(2)}) copy-start(bf16[4,256,2,128]{3,1,2,0:T(8,128)(2,1)S(1)} %fusion.125) | copy-start | bytes 1572868 | tf_op jit(solution)/shard_map/while
  154.4 2.5 %copy-start.6 = (bf16[4,256,2,128]{3,1,2,0:T(8,128)(2,1)S(1)}, bf16[4,256,2,128]{3,1,2,0:T(8,128)(2,1)}, u32[]{:S(2)}) copy-start(bf16[4,256,2,128]{3,1,2,0:T(8,128)(2,1)} %get-tuple-element.906) | copy-start | bytes 1572868 | tf_op jit(solution)/shard_map/while
  157.7 2.0 copy-start.7
  159.8 14.5 %copy-start.8 = (bf16[4,256,2,128]{3,1,2,0:T(8,128)(2,1)S(1)}, bf16[4,256,2,128]{3,1,2,0:T(8,128)(2,1)}, u32[]{:S(2)}) copy-start(bf16[4,256,2,128]{3,1,2,0:T(8,128)(2,1)} %get-tuple-element.213) | copy-start | bytes 1572868
  174.3 61.6 %reduce-scatter.7.cloned.1.call-start = ((), (), s32[]{:S(2)}) async-start(), calls=%async_computation.6 | async-start | bytes 442368
  (7 other events, 8.3 us)
Sparse Core Ops, SparseCore 0:
  174.4 30.2 reduce-scatter.8
  207.0 28.7 reduce-scatter.6
where the time goes:
time: 246 us; the launch traced here: 244 us
  matrix products  54.8 us (22%)
  blocking collectives  51.6 us (21%)
  waiting for transfers between devices  45.2 us (18%)
  local copies, waits for them, and re-layouts  37.3 us (15%)
  other arithmetic  32.1 us (13%)
  between operations  14.3 us (6%)
  starting transfers between devices  7.96 us (3%)
    unnamed x4, waiting for transfers between devices  45.2 us
    all_gather x1, blocking collectives, per_device(): lax.all_gather(prompt_key, 'cand', axis=0, tiled=True)  16.6 us
    dot_general x4, matrix products, forward(): jnp.einsum('hgrj,jhd->rhgd', probs_bf, block_items[1], preferred_element_...  16.5 us
    all_gather x1, blocking collectives, per_device(): lax.all_gather(shared_prompt_value, 'cand', axis=0, tiled=True)  14.6 us
    dot_general x8, matrix products, scores(): jnp.einsum('rhgd,jhd->hgrj', query_heads, key_block, preferred_element_ty...  13.1 us
    unnamed x27, local copies, waits for them, and re-layouts  12.7 us
    all_to_all x1, blocking collectives, per_device(): lax.all_to_all(prompt_values_part.reshape(prefix_count, block_rows, 1, lo...  11.6 us
    and x12, other arithmetic, scores(): visible_mask = (row_valid[:, None] & (prompt_ok | cont_ok))[None, None]  9.99 us
  transfers between devices with their start and end apart: 4, of which 2 were waited for; matrix products, arithmetic and copies ran while one was open for 10% of the time, Pallas kernels for 0%

commit v1 on v0

v1 whole, which is shorter than its diff:
```python
import functools
import math

import jax
import jax.numpy as jnp
from jax import lax
from jax.experimental import pallas as pl
from jax.experimental.pallas import tpu as pltpu
from jax.sharding import PartitionSpec as P

HEAD_WIDTH = 128
MASKED_SCORE = -1e30
F32 = jnp.float32
BF16 = jnp.bfloat16
VMEM_BYTES = 48 * 1024 * 1024
DIMS_NT = (((1,), (1,)), ((), ()))
DIMS_NN = (((1,), (0,)), ((), ()))


def vmem_spec():
    return pl.BlockSpec(memory_space=pltpu.VMEM)


def smem_spec():
    return pl.BlockSpec(memory_space=pltpu.SMEM)


def glue_call(body, out_shape, operands, scalars=1, name=None):
    return pl.pallas_call(
        body,
        out_shape=out_shape,
        in_specs=[smem_spec()] * scalars + [vmem_spec()] * (len(operands) - scalars),
        out_specs=[vmem_spec()] * len(out_shape),
        compiler_params=pltpu.CompilerParams(vmem_limit_bytes=VMEM_BYTES),
        name=name,
    )(*operands)


def split_heads(where, prompt_key, prompt_value, parts, width):
    rows = prompt_key.shape[0]

    def body(where_ref, key_ref, value_ref, *out_refs):
        for step in range(parts):
            target = lax.rem(where_ref[0] + step, parts)
            columns = pl.ds(pl.multiple_of(target * width, width), width)
            out_refs[step][:, :width] = key_ref[:, columns]
            out_refs[step][:, width:] = value_ref[:, columns]

    shapes = [jax.ShapeDtypeStruct((rows, 2 * width), BF16)] * parts
    return glue_call(body, shapes, (where, prompt_key, prompt_value), name="split_heads")


def join_rows(pieces):
    rows, width = pieces[0].shape

    def body(*refs):
        out_ref = refs[-1]
        out_ref[...] = jnp.concatenate(
            [ref[...].astype(F32) for ref in refs[:-1]], axis=0
        ).astype(BF16)

    shapes = [jax.ShapeDtypeStruct((rows * len(pieces), width), BF16)]
    return glue_call(body, shapes, tuple(pieces), scalars=0, name="join_rows")[0]


def add_sibling(kept, arrived):
    chips, rows, width = kept.shape

    def body(kept_ref, arrived_ref, *out_refs):
        for step in range(chips):
            out_refs[step][...] = (
                kept_ref[step].astype(F32) + arrived_ref[step].astype(F32)
            ).astype(BF16)

    shapes = [jax.ShapeDtypeStruct((rows, width), BF16)] * chips
    return glue_call(body, shapes, (kept, arrived), scalars=0, name="add_sibling")


def add_chips(pieces, parts):
    rows, width = pieces[0].shape
    own = rows // parts

    def body(*refs):
        count = len(pieces)
        total = refs[0][...].astype(F32)
        for ref in refs[1:count]:
            total = total + ref[...].astype(F32)
        for step in range(parts):
            refs[count + step][...] = total[step * own : (step + 1) * own].astype(BF16)

    shapes = [jax.ShapeDtypeStruct((own, width), BF16)] * parts
    return glue_call(body, shapes, tuple(pieces), scalars=0, name="add_chips")


def merge_heads(where, pieces):
    rows, double = pieces[0].shape
    width = double // 2
    parts = len(pieces)

    def body(where_ref, *refs):
        key_ref, value_ref = refs[-2:]
        for step in range(parts):
            source = lax.rem(where_ref[0] + parts - step, parts)
            columns = pl.ds(pl.multiple_of(source * width, width), width)
            key_ref[:, columns] = refs[step][:, :width]
            value_ref[:, columns] = refs[step][:, width:]

    shapes = [jax.ShapeDtypeStruct((rows, width * parts), BF16)] * 2
    return glue_call(body, shapes, (where, *pieces), name="merge_heads")


def attention_body(
    prefix_count,
    cand_count,
    own_rows,
    window,
    per_device,
    heads,
    group,
    where_ref,
    assign_ref,
    lengths_ref,
    offsets_ref,
    *refs,
):
    chips = cand_count // 2
    pieces = refs[:cand_count]
    q_ref, g_ref, ck_ref, cv_ref = refs[cand_count : cand_count + 4]
    dq_ref, dck_ref, dcv_ref, keep_ref, send_ref = refs[cand_count + 4 : cand_count + 9]
    (
        table,
        stage,
        keys,
        values,
        keys_t,
        score,
        dprob,
        expo,
        sgrad,
        acc,
        cacc_k,
        cacc_v,
    ) = refs[cand_count + 9 :]
    head = pl.program_id(0)
    win = pl.program_id(1)
    windows = pl.num_programs(1)
    prompt_len = keys.shape[1]
    half = prompt_len // 2
    chunk = math.gcd(half, 128)
    band = 2 * window
    lanes = group * window
    groups = q_ref.shape[1] // HEAD_WIDTH // group
    scale = 1.0 / math.sqrt(HEAD_WIDTH)
    my_prefix = where_ref[0]
    my_cand = where_ref[1]
    width = heads * HEAD_WIDTH

    def token_base(prefix_index, cand_index):
        return pl.multiple_of((prefix_index * cand_count + cand_index) * own_rows, 8)

    @pl.when((head == 0) & (win == 0))
    def _():
        def visit(k, carry):
            count, place = carry
            mine = assign_ref[k] == my_cand

            @pl.when(mine)
            def _():
                table[0, count] = place
                table[1, count] = place + lengths_ref[k]
                table[2, count] = offsets_ref[k]

            return (
                count + mine.astype(jnp.int32),
                place + jnp.where(mine, lengths_ref[k], 0),
            )

        lax.fori_loop(
            0, assign_ref.shape[0], visit, (jnp.int32(0), jnp.int32(0))
        )
        sibling = my_cand + 1 - 2 * lax.rem(my_cand, 2)
        for side, base_cand in ((0, my_cand), (1, sibling)):
            for step in range(chips):
                source = lax.rem(base_cand + 2 * (chips - step), cand_count)
                block = pieces[side * chips + step][...].astype(F32)
                for turn in range(prefix_count):
                    origin = lax.rem(my_prefix + prefix_count - turn, prefix_count)
                    stage[pl.ds(token_base(origin, source), own_rows), :] = block[
                        turn * own_rows : (turn + 1) * own_rows
                    ]
        for h in range(heads):
            k_block = stage[:, h * HEAD_WIDTH : (h + 1) * HEAD_WIDTH]
            keys[h] = k_block.astype(BF16)
            keys_t[h] = k_block.T.astype(BF16)
            values[h] = stage[:, width + h * HEAD_WIDTH : width + (h + 1) * HEAD_WIDTH].astype(
                BF16
            )

    @pl.when(win == 0)
    def _():
        acc[...] = jnp.zeros_like(acc)
        cacc_k[...] = jnp.zeros_like(cacc_k)
        cacc_v[...] = jnp.zeros_like(cacc_v)

    first_row = win * window
    filled = table[1, per_device - 1]

    @pl.when(first_row >= filled)
    def _():
        dq_ref[...] = jnp.zeros_like(dq_ref)

    @pl.when(first_row < filled)
    def _():
        band_row = pl.multiple_of(jnp.maximum(first_row - window, 0), window)
        row = first_row + lax.broadcasted_iota(jnp.int32, (1, lanes), 1) % window
        offset = jnp.zeros((1, lanes), jnp.int32)
        start = jnp.full((1, lanes), windows * window, jnp.int32)
        for c in range(per_device):
            inside = (row >= table[0, c]) & (row < table[1, c])
            offset = jnp.where(inside, table[2, c], offset)
            start = jnp.where(inside, table[0, c], start)
        valid = row < filled
        blocks = [(i * chunk, chunk) for i in range(prompt_len // chunk)]

        def masked(s, first):
            if first < half:
                return s
            place = first + lax.broadcasted_iota(jnp.int32, s.shape, 0)
            return jnp.where(place < offset, s, MASKED_SCORE)

        cont_place = band_row + lax.broadcasted_iota(jnp.int32, (band, lanes), 0)
        cont_seen = (cont_place >= start) & (cont_place <= row)
        ck = ck_ref[pl.ds(band_row, band), :]
        cv = cv_ref[pl.ds(band_row, band), :]

        def fold(x, op):
            return op(x.reshape(x.shape[0] // 8, 8, x.shape[1]), axis=0)

        def rows_of(ref, index):
            return jnp.concatenate(
                [
                    ref[:, (index * group + h) * HEAD_WIDTH : (index * group + h + 1) * HEAD_WIDTH]
                    for h in range(group)
                ],
                axis=0,
            )

        factor = scale * math.log2(math.e)
        scaled_q, scaled_g = [], []
        for index in range(groups):
            q = rows_of(q_ref, index)
            g = rows_of(g_ref, index)
            cols = slice(index * lanes, (index + 1) * lanes)
            top = jnp.full((8, lanes), MASKED_SCORE, F32)
            for first, size in blocks:
                s = lax.dot_general(
                    keys[head, first : first + size], q, DIMS_NT, preferred_element_type=F32
                )
                s = masked(s * factor, first)
                score[first : first + size, cols] = s
                top = jnp.maximum(top, fold(s, jnp.max))
            s = lax.dot_general(ck, q, DIMS_NT, preferred_element_type=F32)
            s = jnp.where(cont_seen, s * factor, MASKED_SCORE)
            score[prompt_len:, cols] = s
            top = jnp.maximum(top, fold(s, jnp.max))
            top = jnp.max(top, axis=0, keepdims=True)
            total = jnp.zeros((8, lanes), F32)
            delta = jnp.zeros((8, lanes), F32)
            for first, size in blocks + [(prompt_len, band)]:
                v = values[head, first : first + size] if first < prompt_len else cv
                dp = lax.dot_general(v, g, DIMS_NT, preferred_element_type=F32)
                e = jnp.exp2(score[first : first + size, cols] - top)
                dprob[first : first + size, cols] = dp
                expo[first : first + size, cols] = e.astype(BF16)
                total = total + fold(e, jnp.sum)
                delta = delta + fold(e * dp, jnp.sum)
            total = jnp.sum(total, axis=0, keepdims=True)
            delta = jnp.sum(delta, axis=0, keepdims=True)
            inverse = jnp.where(valid, 1.0 / total, 0.0)
            delta = delta / total
            for first, size in blocks + [(prompt_len, band)]:
                e = expo[first : first + size, cols].astype(F32)
                sgrad[first : first + size, cols] = (
                    e * (dprob[first : first + size, cols] - delta)
                ).astype(BF16)
            column = jnp.broadcast_to(inverse, (HEAD_WIDTH, lanes)).T
            scaled_q.append((q.astype(F32) * (column * scale)).astype(BF16))
            scaled_g.append((g.astype(F32) * column).astype(BF16))
            dq_t = lax.dot_general(
                keys_t[head], sgrad[:prompt_len, cols], DIMS_NN, preferred_element_type=F32
            ) + lax.dot_general(
                ck.astype(F32).T.astype(BF16),
                sgrad[prompt_len:, cols],
                DIMS_NN,
                preferred_element_type=F32,
            )
            dq = (dq_t * (inverse * scale)).T.astype(BF16)
            for h in range(group):
                place = (index * group + h) * HEAD_WIDTH
                dq_ref[:, place : place + HEAD_WIDTH] = dq[h * window : (h + 1) * window]
        q_all = jnp.concatenate(scaled_q, axis=0)
        g_all = jnp.concatenate(scaled_g, axis=0)
        acc[:, :HEAD_WIDTH] += lax.dot_general(
            sgrad[:prompt_len, :], q_all, DIMS_NN, preferred_element_type=F32
        )
        acc[:, HEAD_WIDTH:] += lax.dot_general(
            expo[:prompt_len, :], g_all, DIMS_NN, preferred_element_type=F32
        )
        cacc_k[pl.ds(band_row, band), :] += lax.dot_general(
            sgrad[prompt_len:, :], q_all, DIMS_NN, preferred_element_type=F32
        )
        cacc_v[pl.ds(band_row, band), :] += lax.dot_general(
            expo[prompt_len:, :], g_all, DIMS_NN, preferred_element_type=F32
        )

    @pl.when(win == windows - 1)
    def _():
        dck_ref[...] = cacc_k[...].astype(BF16)
        dcv_ref[...] = cacc_v[...].astype(BF16)
        sibling = my_cand + 1 - 2 * lax.rem(my_cand, 2)
        for out_ref, base_cand in ((keep_ref, my_cand), (send_ref, sibling)):
            for step in range(chips):
                target = lax.rem(base_cand + 2 * step, cand_count)
                block = jnp.concatenate(
                    [
                        acc[
                            pl.ds(
                                token_base(lax.rem(my_prefix + turn, prefix_count), target),
                                own_rows,
                            ),
                            :,
                        ]
                        for turn in range(prefix_count)
                    ],
                    axis=0,
                ).astype(BF16)
                for h in range(heads):

                    @pl.when(head == h)
                    def _(block=block, h=h, step=step, out_ref=out_ref):
                        out_ref[step, :, h * HEAD_WIDTH : (h + 1) * HEAD_WIDTH] = block[
                            :, :HEAD_WIDTH
                        ]
                        out_ref[
                            step, :, width + h * HEAD_WIDTH : width + (h + 1) * HEAD_WIDTH
                        ] = block[:, HEAD_WIDTH:]


def attention(
    where, assign, lengths, offsets, pieces, query, grad_out, cont_key, cont_value, axes
):
    prefix_count, cand_count = axes
    rows, query_width = query.shape
    heads = cont_key.shape[1] // HEAD_WIDTH
    head_columns = query_width // heads
    per_device = assign.shape[0] // cand_count
    window = rows // per_device
    piece_rows, piece_width = pieces[0].shape
    own_rows = piece_rows // prefix_count
    prompt_len = piece_rows * cand_count
    group = min(max(256 // window, 1), head_columns // HEAD_WIDTH)
    all_lanes = head_columns // HEAD_WIDTH * window
    joined = prompt_len + 2 * window
    chips = cand_count // 2
    by_window = pl.BlockSpec((window, head_columns), lambda h, w, *_: (w, h))
    by_head = pl.BlockSpec((rows, HEAD_WIDTH), lambda h, w, *_: (0, h))
    whole_piece = pl.BlockSpec((piece_rows, piece_width), lambda h, w, *_: (0, 0))
    parts_spec = pl.BlockSpec((chips, piece_rows, piece_width), lambda h, w, *_: (0, 0, 0))
    flops = 10 * query.size * joined
    return pl.pallas_call(
        functools.partial(
            attention_body,
            prefix_count,
            cand_count,
            own_rows,
            window,
            per_device,
            heads,
            group,
        ),
        grid_spec=pltpu.PrefetchScalarGridSpec(
            num_scalar_prefetch=4,
            grid=(heads, per_device),
            in_specs=[whole_piece] * cand_count + [by_window, by_window, by_head, by_head],
            out_specs=[by_window, by_head, by_head, parts_spec, parts_spec],
            scratch_shapes=[
                pltpu.SMEM((3, per_device), jnp.int32),
                pltpu.VMEM((prompt_len, piece_width), F32),
                pltpu.VMEM((heads, prompt_len, HEAD_WIDTH), BF16),
                pltpu.VMEM((heads, prompt_len, HEAD_WIDTH), BF16),
                pltpu.VMEM((heads, HEAD_WIDTH, prompt_len), BF16),
                pltpu.VMEM((joined, all_lanes), F32),
                pltpu.VMEM((joined, all_lanes), F32),
                pltpu.VMEM((joined, all_lanes), BF16),
                pltpu.VMEM((joined, all_lanes), BF16),
                pltpu.VMEM((prompt_len, 2 * HEAD_WIDTH), F32),
                pltpu.VMEM((rows, HEAD_WIDTH), F32),
                pltpu.VMEM((rows, HEAD_WIDTH), F32),
            ],
        ),
        out_shape=[
            jax.ShapeDtypeStruct(query.shape, BF16),
            jax.ShapeDtypeStruct(cont_key.shape, BF16),
            jax.ShapeDtypeStruct(cont_value.shape, BF16),
            jax.ShapeDtypeStruct((chips, piece_rows, piece_width), BF16),
            jax.ShapeDtypeStruct((chips, piece_rows, piece_width), BF16),
        ],
        compiler_params=pltpu.CompilerParams(
            dimension_semantics=("arbitrary", "arbitrary"), vmem_limit_bytes=VMEM_BYTES
        ),
        cost_estimate=pl.CostEstimate(
            flops=flops, bytes_accessed=8 * query.size, transcendentals=query.size * 4
        ),
        name="attention_backward",
    )(where, assign, lengths, offsets, *pieces, query, grad_out, cont_key, cont_value)


def per_device(
    query,
    grad_out,
    continuation_key,
    continuation_value,
    prompt_key,
    shared_prompt_value,
    assign,
    lengths,
    offsets,
):
    prefix_count = lax.axis_size("prefix")
    cand_count = lax.axis_size("cand")
    chips = cand_count // 2
    where = jnp.stack([lax.axis_index("prefix"), lax.axis_index("cand")]).astype(jnp.int32)
    local_width = prompt_key.shape[1] // prefix_count

    def along_prefix(x, step):
        return lax.ppermute(
            x, "prefix", [(i, (i + step) % prefix_count) for i in range(prefix_count)]
        )

    def along_chips(x, step):
        return lax.ppermute(
            x, "cand", [(i, (i + 2 * step) % cand_count) for i in range(cand_count)]
        )

    def to_sibling(x):
        return lax.ppermute(x, "cand", [(i, i ^ 1) for i in range(cand_count)])

    split = split_heads(where, prompt_key, shared_prompt_value, prefix_count, local_width)
    held = join_rows([split[0]] + [along_prefix(split[d], d) for d in range(1, prefix_count)])
    same_core = [held] + [along_chips(held, d) for d in range(1, chips)]
    other_core = [to_sibling(x) for x in same_core]
    query_grad, cont_key_grad, cont_value_grad, kept, sent = attention(
        where,
        assign,
        lengths,
        offsets,
        same_core + other_core,
        query,
        grad_out,
        continuation_key,
        continuation_value,
        (prefix_count, cand_count),
    )
    by_chip = add_sibling(kept, to_sibling(sent))
    split_sums = add_chips(
        [by_chip[0]] + [along_chips(by_chip[d], d) for d in range(1, chips)], prefix_count
    )
    prompt_key_grad, prompt_value_grad = merge_heads(
        where, [split_sums[0]] + [along_prefix(split_sums[d], d) for d in range(1, prefix_count)]
    )
    return (query_grad, cont_key_grad, cont_value_grad, prompt_key_grad, prompt_value_grad)


def solution(mesh):
    in_specs = (
        P("cand", "prefix"),
        P("cand", "prefix"),
        P("cand", "prefix"),
        P("cand", "prefix"),
        P(("prefix", "cand"), None),
        P(("prefix", "cand"), None),
        P(),
        P(),
        P(),
    )
    out_specs = (
        P("cand", "prefix"),
        P("cand", "prefix"),
        P("cand", "prefix"),
        P(("prefix", "cand"), None),
        P(("prefix", "cand"), None),
    )
    return jax.shard_map(
        per_device, mesh=mesh, in_specs=in_specs, out_specs=out_specs, check_vma=False
    )
```

time: 246 us -> 67.2 us (0.27)
  matrix products: 54.8 us -> 0 us
  blocking collectives: 51.6 us -> 0 us
  local copies, waits for them, and re-layouts: 37.3 us -> 4.06 us
  other arithmetic: 32.1 us -> 0.08 us
  waiting for transfers between devices: 45.2 us -> 21.8 us
  starting transfers between devices: 7.96 us -> 25.7 us
  Pallas kernels: 0 us -> 14.5 us
  between operations: 14.3 us -> 0.71 us
    dot_general x28 -> x0, matrix products: 54.8 us -> none  [the longest x4 16.5 us: forward(): jnp.einsum('hgrj,jhd->rhgd', probs_bf, block_items[1], preferred_element_...]
    unnamed x4 -> x0, waiting for transfers between devices: 45.2 us -> none
    all_gather x2 -> x0, blocking collectives: 31.2 us -> none  [the longest x1 16.6 us: per_device(): lax.all_gather(prompt_key, 'cand', axis=0, tiled=True)]
    ppermute x0 -> x17, starting transfers between devices: none -> 25.7 us  [the longest x6 9.13 us: along_prefix(): lax.ppermute(x, 'prefix', [(i, (i + step) % prefix_count) for i in range(...]
    ppermute x0 -> x17, waiting for transfers between devices: none -> 21.8 us  [the longest x6 13.8 us: along_chips(): lax.ppermute(x, 'cand', [(i, (i + 2 * step) % cand_count) for i in range(...]
    all_to_all x2 -> x0, blocking collectives: 20.4 us -> none  [the longest x1 11.6 us: per_device(): lax.all_to_all(prompt_values_part.reshape(prefix_count, block_rows, 1, lo...]
    pallas_call x0 -> x6, Pallas kernels: none -> 14.5 us  [the longest x1 12.6 us: attention(): pl.pallas_call(functools.partial(attention_body, prefix_count, cand_count...]
    and x12 -> x0, other arithmetic: 9.99 us -> none  [scores(): visible_mask = (row_valid[:, None] & (prompt_ok | cont_ok))[None, None]]
  transfers between devices with their start and end apart: 4 -> 17, of which waited for: 2 -> 12; matrix products, arithmetic and copies ran while one was open for 10% -> 0% of each run, Pallas kernels for 0% -> 0%
where the time goes in v1:
time: 67.2 us; the launch traced here: 66.9 us
  starting transfers between devices  25.7 us (38%)
  waiting for transfers between devices  21.8 us (32%)
  Pallas kernels  14.5 us (22%)
  local copies, waits for them, and re-layouts  4.06 us (6%)
  between operations  0.71 us (1%)
    ppermute x6, waiting for transfers between devices, along_chips(): lax.ppermute(x, 'cand', [(i, (i + 2 * step) % cand_count) for i in range(...  13.8 us
    pallas_call x1, Pallas kernels, attention(): pl.pallas_call(functools.partial(attention_body, prefix_count, cand_count...  12.6 us
    ppermute x6, starting transfers between devices, along_prefix(): lax.ppermute(x, 'prefix', [(i, (i + step) % prefix_count) for i in range(...  9.13 us
    ppermute x6, starting transfers between devices, along_chips(): lax.ppermute(x, 'cand', [(i, (i + 2 * step) % cand_count) for i in range(...  8.55 us
    ppermute x5, starting transfers between devices, to_sibling(): return lax.ppermute(x, 'cand', [(i, i ^ 1) for i in range(cand_count)])  8.05 us
    ppermute x6, waiting for transfers between devices, along_prefix(): lax.ppermute(x, 'prefix', [(i, (i + step) % prefix_count) for i in range(...  5.68 us
    unnamed x18, local copies, waits for them, and re-layouts  4.06 us
    ppermute x5, waiting for transfers between devices, to_sibling(): return lax.ppermute(x, 'cand', [(i, i ^ 1) for i in range(cand_count)])  2.29 us
  transfers between devices with their start and end apart: 17, of which 12 were waited for; matrix products, arithmetic and copies ran while one was open for 0% of the time, Pallas kernels for 0%

profile of v1, /device:TPU:0, one launch (start us, length us, event | category | flops | bytes accessed | tf_op | source)
XLA Modules:
  0.0 66.9 jit_solution(2525141135676909267)
XLA Ops:
  0.6 0.1 pad_add_fusion.where_ref
  0.7 0.8 %copy-done = bf16[24,1024]{1,0:T(8,128)(2,1)S(1)} copy-done((bf16[24,1024]{1,0:T(8,128)(2,1)S(1)}, bf16[24,1024]{1,0:T(8,128)(2,1)}, u32[]{:S(2)}) %copy-start) | copy-done | bytes 49176
  1.5 0.8 %copy-done.1 = bf16[24,1024]{1,0:T(8,128)(2,1)S(1)} copy-done((bf16[24,1024]{1,0:T(8,128)(2,1)S(1)}, bf16[24,1024]{1,0:T(8,128)(2,1)}, u32[]{:S(2)}) %copy-start.1) | copy-done | bytes 49176
  2.3 0.6 split_heads.1
  2.9 3.0 %collective-permute-start = (bf16[24,512]{1,0:T(8,128)(2,1)S(1)}, bf16[24,512]{1,0:T(8,128)(2,1)S(1)}, u32[]{:S(2)}, u32[]{:S(2)}) collective-permute-start(bf16[24,512]{1,0:T(8,128)(2,1)S(1)} %get-tuple-element.25), channel_id=1, source_target_pairs={{0,8},{8,16},{16,24},{24,0},{1,9},{9,17},{17,25},{25,1},{2,10},{10... | collective-permute-start | bytes 73736 | tf_op jit(solution)/shard_map/ppermute | solution.py:436
  5.9 1.5 %collective-permute-start.1 = (bf16[24,512]{1,0:T(8,128)(2,1)S(1)}, bf16[24,512]{1,0:T(8,128)(2,1)S(1)}, u32[]{:S(2)}, u32[]{:S(2)}) collective-permute-start(bf16[24,512]{1,0:T(8,128)(2,1)S(1)} %get-tuple-element.26), channel_id=1, source_target_pairs={{0,16},{8,24},{16,0},{24,8},{1,17},{9,25},{17,1},{25,9},{2,18},{10... | collective-permute-start | bytes 73736 | tf_op jit(solution)/shard_map/ppermute | solution.py:436
  7.4 1.4 %collective-permute-start.2 = (bf16[24,512]{1,0:T(8,128)(2,1)S(1)}, bf16[24,512]{1,0:T(8,128)(2,1)S(1)}, u32[]{:S(2)}, u32[]{:S(2)}) collective-permute-start(bf16[24,512]{1,0:T(8,128)(2,1)S(1)} %get-tuple-element.27), channel_id=1, source_target_pairs={{0,24},{8,0},{16,8},{24,16},{1,25},{9,1},{17,9},{25,17},{2,26},{10... | collective-permute-start | bytes 73736 | tf_op jit(solution)/shard_map/ppermute | solution.py:436
  8.8 0.9 %collective-permute-done.1.refs_2_ = bf16[24,512]{1,0:T(8,128)(2,1)S(1)} collective-permute-done((bf16[24,512]{1,0:T(8,128)(2,1)S(1)}, bf16[24,512]{1,0:T(8,128)(2,1)S(1)}, u32[]{:S(2)}, u32[]{:S(2)}) %collective-permute-start.1) | collective-permute-done | bytes 24608 | tf_op jit(solution)/shard_map/ppermute | solution.py:436
  9.7 1.5 %collective-permute-done.2.refs_3_ = bf16[24,512]{1,0:T(8,128)(2,1)S(1)} collective-permute-done((bf16[24,512]{1,0:T(8,128)(2,1)S(1)}, bf16[24,512]{1,0:T(8,128)(2,1)S(1)}, u32[]{:S(2)}, u32[]{:S(2)}) %collective-permute-start.2) | collective-permute-done | bytes 24608 | tf_op jit(solution)/shard_map/ppermute | solution.py:436
  11.2 3.7 %collective-permute-start.5 = (bf16[96,512]{1,0:T(8,128)(2,1)S(1)}, bf16[96,512]{1,0:T(8,128)(2,1)S(1)}, u32[]{:S(2)}, u32[]{:S(2)}) collective-permute-start(bf16[96,512]{1,0:T(8,128)(2,1)S(1)} %join_rows.1.refs_0_), channel_id=1, source_target_pairs={{0,6},{1,7},{2,0},{3,1},{4,2},{5,3},{6,4},{7,5},{8,14},{9,15},{10,... | collective-permute-start | bytes 294920 | tf_op jit(solution)/shard_map/ppermute | solution.py:441
  14.9 1.0 %collective-permute-start.3 = (bf16[96,512]{1,0:T(8,128)(2,1)S(1)}, bf16[96,512]{1,0:T(8,128)(2,1)S(1)}, u32[]{:S(2)}, u32[]{:S(2)}) collective-permute-start(bf16[96,512]{1,0:T(8,128)(2,1)S(1)} %join_rows.1.refs_0_), channel_id=1, source_target_pairs={{0,2},{1,3},{2,4},{3,5},{4,6},{5,7},{6,0},{7,1},{8,10},{9,11},{10,... | collective-permute-start | bytes 294920 | tf_op jit(solution)/shard_map/ppermute | solution.py:441
  15.9 1.8 %collective-permute-done.5.refs_3_ = bf16[96,512]{1,0:T(8,128)(2,1)S(1)} collective-permute-done((bf16[96,512]{1,0:T(8,128)(2,1)S(1)}, bf16[96,512]{1,0:T(8,128)(2,1)S(1)}, u32[]{:S(2)}, u32[]{:S(2)}) %collective-permute-start.5) | collective-permute-done | bytes 98336 | tf_op jit(solution)/shard_map/ppermute | solution.py:441
  17.7 5.1 %collective-permute-done.4.refs_2_ = bf16[96,512]{1,0:T(8,128)(2,1)S(1)} collective-permute-done((bf16[96,512]{1,0:T(8,128)(2,1)S(1)}, bf16[96,512]{1,0:T(8,128)(2,1)S(1)}, u32[]{:S(2)}, u32[]{:S(2)}) %collective-permute-start.4) | collective-permute-done | bytes 98336 | tf_op jit(solution)/shard_map/ppermute | solution.py:441
  22.8 0.5 collective-permute-start.7
  23.3 0.8 %collective-permute-done.8.refs_6_ = bf16[96,512]{1,0:T(8,128)(2,1)S(1)} collective-permute-done((bf16[96,512]{1,0:T(8,128)(2,1)S(1)}, bf16[96,512]{1,0:T(8,128)(2,1)S(1)}, u32[]{:S(2)}, u32[]{:S(2)}) %collective-permute-start.8) | collective-permute-done | bytes 98336 | tf_op jit(solution)/shard_map/ppermute | solution.py:446
  24.1 0.2 collective-permute-done.7.refs_5_
  24.3 1.2 %copy-done.2 = bf16[256,2048]{1,0:T(8,128)(2,1)S(1)} copy-done((bf16[256,2048]{1,0:T(8,128)(2,1)S(1)}, bf16[256,2048]{1,0:T(8,128)(2,1)}, u32[]{:S(2)}) %copy-start.2) | copy-done | bytes 1048600
  25.5 1.2 %copy-done.3 = bf16[256,2048]{1,0:T(8,128)(2,1)S(1)} copy-done((bf16[256,2048]{1,0:T(8,128)(2,1)S(1)}, bf16[256,2048]{1,0:T(8,128)(2,1)}, u32[]{:S(2)}) %copy-start.3) | copy-done | bytes 1048600
  26.7 12.6 %attention_backward.1 = (bf16[256,2048]{1,0:T(8,128)(2,1)}, bf16[256,256]{1,0:T(8,128)(2,1)}, bf16[256,256]{1,0:T(8,128)(2,1)}, bf16[4,96,512]{2,1,0:T(8,128)(2,1)S(1)}, bf16[4,96,512]{2,1,0:T(8,128)(2,1)S(1)}) custom-call(s32[2]{0:T(128)S(1)} %pad_add_fusion.where_ref, s32[32]{0:T(128)S(1)} %copy-done.6, s32[32]{0:T(128)S(1)} %copy-done.7, ...), custom_call_target="tpu_custom_call" | custom-call | flops 4697620480 | bytes 4194304 | tf_op jit(solution)/shard_map/attention_backward/pallas_call | solution.py:370
  39.3 7.5 %collective-permute-start.10 = (bf16[4,96,512]{2,1,0:T(8,128)(2,1)S(1)}, bf16[4,96,512]{2,1,0:T(8,128)(2,1)S(1)}, u32[]{:S(2)}, u32[]{:S(2)}) collective-permute-start(bf16[4,96,512]{2,1,0:T(8,128)(2,1)S(1)} %get-tuple-element.32), channel_id=1, source_target_pairs={{0,1},{1,0},{2,3},{3,2},{4,5},{5,4},{6,7},{7,6},{8,9},{9,8},{10,11... | collective-permute-start | bytes 1179656 | tf_op jit(solution)/shard_map/ppermute | solution.py:446
  46.8 1.3 %collective-permute-done.10.arrived_ref = bf16[4,96,512]{2,1,0:T(8,128)(2,1)S(1)} collective-permute-done((bf16[4,96,512]{2,1,0:T(8,128)(2,1)S(1)}, bf16[4,96,512]{2,1,0:T(8,128)(2,1)S(1)}, u32[]{:S(2)}, u32[]{:S(2)}) %collective-permute-start.10) | collective-permute-done | bytes 393248 | tf_op jit(solution)/shard_map/ppermute | solution.py:446
  48.2 0.1 add_sibling.1
  48.4 3.7 %collective-permute-start.13 = (bf16[96,512]{1,0:T(8,128)(2,1)S(1)}, bf16[96,512]{1,0:T(8,128)(2,1)S(1)}, u32[]{:S(2)}, u32[]{:S(2)}) collective-permute-start(bf16[96,512]{1,0:T(8,128)(2,1)S(1)} %get-tuple-element.36), channel_id=1, source_target_pairs={{0,6},{1,7},{2,0},{3,1},{4,2},{5,3},{6,4},{7,5},{8,14},{9,15},{10,... | collective-permute-start | bytes 294920 | tf_op jit(solution)/shard_map/ppermute | solution.py:441
  52.2 3.7 %collective-permute-done.11.refs_1_ = bf16[96,512]{1,0:T(8,128)(2,1)S(1)} collective-permute-done((bf16[96,512]{1,0:T(8,128)(2,1)S(1)}, bf16[96,512]{1,0:T(8,128)(2,1)S(1)}, u32[]{:S(2)}, u32[]{:S(2)}) %collective-permute-start.11) | collective-permute-done | bytes 98336 | tf_op jit(solution)/shard_map/ppermute | solution.py:441
  55.8 3.3 %collective-permute-done.12.refs_2_ = bf16[96,512]{1,0:T(8,128)(2,1)S(1)} collective-permute-done((bf16[96,512]{1,0:T(8,128)(2,1)S(1)}, bf16[96,512]{1,0:T(8,128)(2,1)S(1)}, u32[]{:S(2)}, u32[]{:S(2)}) %collective-permute-start.12) | collective-permute-done | bytes 98336 | tf_op jit(solution)/shard_map/ppermute | solution.py:441
  59.2 1.1 %collective-permute-start.14 = (bf16[24,512]{1,0:T(8,128)(2,1)S(1)}, bf16[24,512]{1,0:T(8,128)(2,1)S(1)}, u32[]{:S(2)}, u32[]{:S(2)}) collective-permute-start(bf16[24,512]{1,0:T(8,128)(2,1)S(1)} %get-tuple-element.38), channel_id=1, source_target_pairs={{0,8},{8,16},{16,24},{24,0},{1,9},{9,17},{17,25},{25,1},{2,10},{10... | collective-permute-start | bytes 73736 | tf_op jit(solution)/shard_map/ppermute | solution.py:436
  60.3 1.5 %collective-permute-start.15 = (bf16[24,512]{1,0:T(8,128)(2,1)S(1)}, bf16[24,512]{1,0:T(8,128)(2,1)S(1)}, u32[]{:S(2)}, u32[]{:S(2)}) collective-permute-start(bf16[24,512]{1,0:T(8,128)(2,1)S(1)} %get-tuple-element.39), channel_id=1, source_target_pairs={{0,16},{8,24},{16,0},{24,8},{1,17},{9,25},{17,1},{25,9},{2,18},{10... | collective-permute-start | bytes 73736 | tf_op jit(solution)/shard_map/ppermute | solution.py:436
  61.8 0.5 collective-permute-start.16
  62.4 1.6 %collective-permute-done.14.refs_1_ = bf16[24,512]{1,0:T(8,128)(2,1)S(1)} collective-permute-done((bf16[24,512]{1,0:T(8,128)(2,1)S(1)}, bf16[24,512]{1,0:T(8,128)(2,1)S(1)}, u32[]{:S(2)}, u32[]{:S(2)}) %collective-permute-start.14) | collective-permute-done | bytes 24608 | tf_op jit(solution)/shard_map/ppermute | solution.py:436
  64.0 0.3 collective-permute-done.15.refs_2_
  64.2 1.4 %collective-permute-done.16.refs_3_ = bf16[24,512]{1,0:T(8,128)(2,1)S(1)} collective-permute-done((bf16[24,512]{1,0:T(8,128)(2,1)S(1)}, bf16[24,512]{1,0:T(8,128)(2,1)S(1)}, u32[]{:S(2)}, u32[]{:S(2)}) %collective-permute-start.16) | collective-permute-done | bytes 24608 | tf_op jit(solution)/shard_map/ppermute | solution.py:436
  65.7 1.2 %merge_heads.1 = (bf16[24,1024]{1,0:T(8,128)(2,1)}, bf16[24,1024]{1,0:T(8,128)(2,1)}) custom-call(s32[2]{0:T(128)S(1)} %pad_add_fusion.where_ref, bf16[24,512]{1,0:T(8,128)(2,1)S(1)} %get-tuple-element.37.refs_0_, bf16[24,512]{1,0:T(8,128)(2,1)S(1)} %collective-permute-done.14.refs_1_, bf16[24,512]{1,0:T(8,128)(2,1)S(1)} %collective-permute-done.15.refs_2_, ...), custom_call_target="tpu_custom_call" | custom-call | tf_op jit(solution)/shard_map/merge_heads/pallas_call | solution.py:29
  (27 shorter events, 0.2 us)
Async XLA Ops:
  0.7 0.8 %copy-start = (bf16[24,1024]{1,0:T(8,128)(2,1)S(1)}, bf16[24,1024]{1,0:T(8,128)(2,1)}, u32[]{:S(2)}) copy-start(bf16[24,1024]{1,0:T(8,128)(2,1)} %key_ref.1) | copy-start | bytes 147460
  1.5 0.8 %copy-start.1 = (bf16[24,1024]{1,0:T(8,128)(2,1)S(1)}, bf16[24,1024]{1,0:T(8,128)(2,1)}, u32[]{:S(2)}) copy-start(bf16[24,1024]{1,0:T(8,128)(2,1)} %value_ref.1) | copy-start | bytes 147460
  2.3 21.9 %copy-start.4 = (bf16[256,256]{1,0:T(8,128)(2,1)S(1)}, bf16[256,256]{1,0:T(8,128)(2,1)}, u32[]{:S(2)}) copy-start(bf16[256,256]{1,0:T(8,128)(2,1)} %refs_10_.1) | copy-start | bytes 393220
  2.3 21.9 %copy-start.5 = (bf16[256,256]{1,0:T(8,128)(2,1)S(1)}, bf16[256,256]{1,0:T(8,128)(2,1)}, u32[]{:S(2)}) copy-start(bf16[256,256]{1,0:T(8,128)(2,1)} %refs_11_.1) | copy-start | bytes 393220
  2.9 5.9 %collective-permute-start = (bf16[24,512]{1,0:T(8,128)(2,1)S(1)}, bf16[24,512]{1,0:T(8,128)(2,1)S(1)}, u32[]{:S(2)}, u32[]{:S(2)}) collective-permute-start(bf16[24,512]{1,0:T(8,128)(2,1)S(1)} %get-tuple-element.25), channel_id=1, source_target_pairs={{0,8},{8,16},{16,24},{24,0},{1,9},{9,17},{17,25},{25,1},{2,10},{10... | collective-permute-start | bytes 73736 | tf_op jit(solution)/shard_map/ppermute | solution.py:436
  5.9 3.8 %collective-permute-start.1 = (bf16[24,512]{1,0:T(8,128)(2,1)S(1)}, bf16[24,512]{1,0:T(8,128)(2,1)S(1)}, u32[]{:S(2)}, u32[]{:S(2)}) collective-permute-start(bf16[24,512]{1,0:T(8,128)(2,1)S(1)} %get-tuple-element.26), channel_id=1, source_target_pairs={{0,16},{8,24},{16,0},{24,8},{1,17},{9,25},{17,1},{25,9},{2,18},{10... | collective-permute-start | bytes 73736 | tf_op jit(solution)/shard_map/ppermute | solution.py:436
  7.4 3.8 %collective-permute-start.2 = (bf16[24,512]{1,0:T(8,128)(2,1)S(1)}, bf16[24,512]{1,0:T(8,128)(2,1)S(1)}, u32[]{:S(2)}, u32[]{:S(2)}) collective-permute-start(bf16[24,512]{1,0:T(8,128)(2,1)S(1)} %get-tuple-element.27), channel_id=1, source_target_pairs={{0,24},{8,0},{16,8},{24,16},{1,25},{9,1},{17,9},{25,17},{2,26},{10... | collective-permute-start | bytes 73736 | tf_op jit(solution)/shard_map/ppermute | solution.py:436
  11.2 13.0 %copy-start.6 = (s32[32]{0:T(128)S(1)}, s32[32]{0:T(128)}, u32[]{:S(2)}) copy-start(s32[32]{0:T(128)} %assign_ref.1) | copy-start | bytes 388
  11.2 13.0 %copy-start.7 = (s32[32]{0:T(128)S(1)}, s32[32]{0:T(128)}, u32[]{:S(2)}) copy-start(s32[32]{0:T(128)} %lengths_ref.1) | copy-start | bytes 388
  11.2 13.0 %copy-start.8 = (s32[32]{0:T(128)S(1)}, s32[32]{0:T(128)}, u32[]{:S(2)}) copy-start(s32[32]{0:T(128)} %offsets_ref.1) | copy-start | bytes 388
  11.2 6.4 %collective-permute-start.5 = (bf16[96,512]{1,0:T(8,128)(2,1)S(1)}, bf16[96,512]{1,0:T(8,128)(2,1)S(1)}, u32[]{:S(2)}, u32[]{:S(2)}) collective-permute-start(bf16[96,512]{1,0:T(8,128)(2,1)S(1)} %join_rows.1.refs_0_), channel_id=1, source_target_pairs={{0,6},{1,7},{2,0},{3,1},{4,2},{5,3},{6,4},{7,5},{8,14},{9,15},{10,... | collective-permute-start | bytes 294920 | tf_op jit(solution)/shard_map/ppermute | solution.py:441
  14.9 7.9 %collective-permute-start.4 = (bf16[96,512]{1,0:T(8,128)(2,1)S(1)}, bf16[96,512]{1,0:T(8,128)(2,1)S(1)}, u32[]{:S(2)}, u32[]{:S(2)}) collective-permute-start(bf16[96,512]{1,0:T(8,128)(2,1)S(1)} %join_rows.1.refs_0_), channel_id=1, source_target_pairs={{0,4},{1,5},{2,6},{3,7},{4,0},{5,1},{6,2},{7,3},{8,12},{9,13},{10,... | collective-permute-start | bytes 294920 | tf_op jit(solution)/shard_map/ppermute | solution.py:441
  14.9 7.9 %collective-permute-start.3 = (bf16[96,512]{1,0:T(8,128)(2,1)S(1)}, bf16[96,512]{1,0:T(8,128)(2,1)S(1)}, u32[]{:S(2)}, u32[]{:S(2)}) collective-permute-start(bf16[96,512]{1,0:T(8,128)(2,1)S(1)} %join_rows.1.refs_0_), channel_id=1, source_target_pairs={{0,2},{1,3},{2,4},{3,5},{4,6},{5,7},{6,0},{7,1},{8,10},{9,11},{10,... | collective-permute-start | bytes 294920 | tf_op jit(solution)/shard_map/ppermute | solution.py:441
  15.9 7.4 %collective-permute-start.6 = (bf16[96,512]{1,0:T(8,128)(2,1)S(1)}, bf16[96,512]{1,0:T(8,128)(2,1)S(1)}, u32[]{:S(2)}, u32[]{:S(2)}) collective-permute-start(bf16[96,512]{1,0:T(8,128)(2,1)S(1)} %join_rows.1.refs_0_), channel_id=1, source_target_pairs={{0,1},{1,0},{2,3},{3,2},{4,5},{5,4},{6,7},{7,6},{8,9},{9,8},{10,11... | collective-permute-start | bytes 294920 | tf_op jit(solution)/shard_map/ppermute | solution.py:446
  17.7 5.6 %collective-permute-start.9 = (bf16[96,512]{1,0:T(8,128)(2,1)S(1)}, bf16[96,512]{1,0:T(8,128)(2,1)S(1)}, u32[]{:S(2)}, u32[]{:S(2)}) collective-permute-start(bf16[96,512]{1,0:T(8,128)(2,1)S(1)} %collective-permute-done.5.refs_3_), channel_id=1, source_target_pairs={{0,1},{1,0},{2,3},{3,2},{4,5},{5,4},{6,7},{7,6},{8,9},{9,8},{10,11... | collective-permute-start | bytes 294920 | tf_op jit(solution)/shard_map/ppermute | solution.py:446
  22.8 1.3 %collective-permute-start.8 = (bf16[96,512]{1,0:T(8,128)(2,1)S(1)}, bf16[96,512]{1,0:T(8,128)(2,1)S(1)}, u32[]{:S(2)}, u32[]{:S(2)}) collective-permute-start(bf16[96,512]{1,0:T(8,128)(2,1)S(1)} %collective-permute-done.4.refs_2_), channel_id=1, source_target_pairs={{0,1},{1,0},{2,3},{3,2},{4,5},{5,4},{6,7},{7,6},{8,9},{9,8},{10,11... | collective-permute-start | bytes 294920 | tf_op jit(solution)/shard_map/ppermute | solution.py:446
  22.8 1.5 %collective-permute-start.7 = (bf16[96,512]{1,0:T(8,128)(2,1)S(1)}, bf16[96,512]{1,0:T(8,128)(2,1)S(1)}, u32[]{:S(2)}, u32[]{:S(2)}) collective-permute-start(bf16[96,512]{1,0:T(8,128)(2,1)S(1)} %collective-permute-done.3.refs_1_), channel_id=1, source_target_pairs={{0,1},{1,0},{2,3},{3,2},{4,5},{5,4},{6,7},{7,6},{8,9},{9,8},{10,11... | collective-permute-start | bytes 294920 | tf_op jit(solution)/shard_map/ppermute | solution.py:446
  24.2 1.2 %copy-start.2 = (bf16[256,2048]{1,0:T(8,128)(2,1)S(1)}, bf16[256,2048]{1,0:T(8,128)(2,1)}, u32[]{:S(2)}) copy-start(bf16[256,2048]{1,0:T(8,128)(2,1)} %refs_8_.1) | copy-start | bytes 3145732
  25.5 1.2 %copy-start.3 = (bf16[256,2048]{1,0:T(8,128)(2,1)S(1)}, bf16[256,2048]{1,0:T(8,128)(2,1)}, u32[]{:S(2)}) copy-start(bf16[256,2048]{1,0:T(8,128)(2,1)} %refs_9_.1) | copy-start | bytes 3145732
  39.3 8.9 %collective-permute-start.10 = (bf16[4,96,512]{2,1,0:T(8,128)(2,1)S(1)}, bf16[4,96,512]{2,1,0:T(8,128)(2,1)S(1)}, u32[]{:S(2)}, u32[]{:S(2)}) collective-permute-start(bf16[4,96,512]{2,1,0:T(8,128)(2,1)S(1)} %get-tuple-element.32), channel_id=1, source_target_pairs={{0,1},{1,0},{2,3},{3,2},{4,5},{5,4},{6,7},{7,6},{8,9},{9,8},{10,11... | collective-permute-start | bytes 1179656 | tf_op jit(solution)/shard_map/ppermute | solution.py:446
  48.3 7.6 %collective-permute-start.11 = (bf16[96,512]{1,0:T(8,128)(2,1)S(1)}, bf16[96,512]{1,0:T(8,128)(2,1)S(1)}, u32[]{:S(2)}, u32[]{:S(2)}) collective-permute-start(bf16[96,512]{1,0:T(8,128)(2,1)S(1)} %get-tuple-element.34), channel_id=1, source_target_pairs={{0,2},{1,3},{2,4},{3,5},{4,6},{5,7},{6,0},{7,1},{8,10},{9,11},{10,... | collective-permute-start | bytes 294920 | tf_op jit(solution)/shard_map/ppermute | solution.py:441
  48.3 10.8 %collective-permute-start.12 = (bf16[96,512]{1,0:T(8,128)(2,1)S(1)}, bf16[96,512]{1,0:T(8,128)(2,1)S(1)}, u32[]{:S(2)}, u32[]{:S(2)}) collective-permute-start(bf16[96,512]{1,0:T(8,128)(2,1)S(1)} %get-tuple-element.35), channel_id=1, source_target_pairs={{0,4},{1,5},{2,6},{3,7},{4,0},{5,1},{6,2},{7,3},{8,12},{9,13},{10,... | collective-permute-start | bytes 294920 | tf_op jit(solution)/shard_map/ppermute | solution.py:441
  48.4 10.7 %collective-permute-start.13 = (bf16[96,512]{1,0:T(8,128)(2,1)S(1)}, bf16[96,512]{1,0:T(8,128)(2,1)S(1)}, u32[]{:S(2)}, u32[]{:S(2)}) collective-permute-start(bf16[96,512]{1,0:T(8,128)(2,1)S(1)} %get-tuple-element.36), channel_id=1, source_target_pairs={{0,6},{1,7},{2,0},{3,1},{4,2},{5,3},{6,4},{7,5},{8,14},{9,15},{10,... | collective-permute-start | bytes 294920 | tf_op jit(solution)/shard_map/ppermute | solution.py:441
  59.2 4.8 %collective-permute-start.14 = (bf16[24,512]{1,0:T(8,128)(2,1)S(1)}, bf16[24,512]{1,0:T(8,128)(2,1)S(1)}, u32[]{:S(2)}, u32[]{:S(2)}) collective-permute-start(bf16[24,512]{1,0:T(8,128)(2,1)S(1)} %get-tuple-element.38), channel_id=1, source_target_pairs={{0,8},{8,16},{16,24},{24,0},{1,9},{9,17},{17,25},{25,1},{2,10},{10... | collective-permute-start | bytes 73736 | tf_op jit(solution)/shard_map/ppermute | solution.py:436
  60.3 3.9 %collective-permute-start.15 = (bf16[24,512]{1,0:T(8,128)(2,1)S(1)}, bf16[24,512]{1,0:T(8,128)(2,1)S(1)}, u32[]{:S(2)}, u32[]{:S(2)}) collective-permute-start(bf16[24,512]{1,0:T(8,128)(2,1)S(1)} %get-tuple-element.39), channel_id=1, source_target_pairs={{0,16},{8,24},{16,0},{24,8},{1,17},{9,25},{17,1},{25,9},{2,18},{10... | collective-permute-start | bytes 73736 | tf_op jit(solution)/shard_map/ppermute | solution.py:436
  61.8 3.8 %collective-permute-start.16 = (bf16[24,512]{1,0:T(8,128)(2,1)S(1)}, bf16[24,512]{1,0:T(8,128)(2,1)S(1)}, u32[]{:S(2)}, u32[]{:S(2)}) collective-permute-start(bf16[24,512]{1,0:T(8,128)(2,1)S(1)} %get-tuple-element.40), channel_id=1, source_target_pairs={{0,24},{8,0},{16,8},{24,16},{1,25},{9,1},{17,9},{25,17},{2,26},{10... | collective-permute-start | bytes 73736 | tf_op jit(solution)/shard_map/ppermute | solution.py:436

commit v2 on v1

v2 whole, which is shorter than its diff:
```python
import functools
import math

import jax
import jax.numpy as jnp
from jax import lax
from jax.experimental import pallas as pl
from jax.experimental.pallas import tpu as pltpu
from jax.sharding import PartitionSpec as P

HEAD_WIDTH = 128
MASKED_SCORE = -1e30
F32 = jnp.float32
BF16 = jnp.bfloat16
VMEM_BYTES = 40 * 1024 * 1024
GLUE_VMEM_BYTES = 8 * 1024 * 1024
DIMS_NT = (((1,), (1,)), ((), ()))
DIMS_NN = (((1,), (0,)), ((), ()))


def vmem_spec():
    return pl.BlockSpec(memory_space=pltpu.VMEM)


def smem_spec():
    return pl.BlockSpec(memory_space=pltpu.SMEM)


def glue_call(body, out_shape, operands, scalars=1, name=None):
    return pl.pallas_call(
        body,
        out_shape=out_shape,
        in_specs=[smem_spec()] * scalars + [vmem_spec()] * (len(operands) - scalars),
        out_specs=[vmem_spec()] * len(out_shape),
        compiler_params=pltpu.CompilerParams(vmem_limit_bytes=GLUE_VMEM_BYTES),
        name=name,
    )(*operands)


def split_heads(prompt_key, prompt_value, parts, chips):
    rows, full = prompt_key.shape
    width = full // parts

    def body(key_hbm, value_hbm, out_ref, key_ref, value_ref, sems):
        copies = [
            pltpu.make_async_copy(key_hbm, key_ref, sems.at[0]),
            pltpu.make_async_copy(value_hbm, value_ref, sems.at[1]),
        ]
        for copy in copies:
            copy.start()
        for copy in copies:
            copy.wait()
        for q in range(parts):
            for z in range(chips):
                out_ref[q * chips + z, :, :width] = key_ref[:, q * width : (q + 1) * width]
                out_ref[q * chips + z, :, width:] = value_ref[:, q * width : (q + 1) * width]

    return pl.pallas_call(
        body,
        out_shape=jax.ShapeDtypeStruct((parts * chips, rows, 2 * width), BF16),
        in_specs=[pl.BlockSpec(memory_space=pl.ANY)] * 2,
        out_specs=vmem_spec(),
        scratch_shapes=[
            pltpu.VMEM(prompt_key.shape, BF16),
            pltpu.VMEM(prompt_value.shape, BF16),
            pltpu.SemaphoreType.DMA((2,)),
        ],
        compiler_params=pltpu.CompilerParams(vmem_limit_bytes=GLUE_VMEM_BYTES),
        name="split_heads",
    )(prompt_key, prompt_value)


def add_sibling(kept, arrived):
    def body(kept_ref, arrived_ref, out_ref):
        for i in range(kept.shape[0]):
            out_ref[i] = (kept_ref[i].astype(F32) + arrived_ref[i].astype(F32)).astype(BF16)

    shapes = [jax.ShapeDtypeStruct(kept.shape, BF16)]
    return glue_call(body, shapes, (kept, arrived), scalars=0, name="add_sibling")[0]


def add_chips(pieces, parts, chips):
    rows, double = pieces.shape[1:]
    width = double // 2

    def body(piece_ref, key_ref, value_ref):
        for p in range(parts):
            total = piece_ref[p * chips].astype(F32)
            for z in range(1, chips):
                total = total + piece_ref[p * chips + z].astype(F32)
            total = total.astype(BF16)
            key_ref[:, p * width : (p + 1) * width] = total[:, :width]
            value_ref[:, p * width : (p + 1) * width] = total[:, width:]

    shapes = [jax.ShapeDtypeStruct((rows, width * parts), BF16)] * 2
    return glue_call(body, shapes, (pieces,), scalars=0, name="add_chips")


def attention_body(
    prefix_count,
    cand_count,
    window,
    per_device,
    heads,
    group,
    where_ref,
    assign_ref,
    lengths_ref,
    offsets_ref,
    own_ref,
    other_ref,
    ck_ref,
    cv_ref,
    q_hbm,
    g_hbm,
    dq_hbm,
    dck_ref,
    dcv_ref,
    keep_ref,
    send_ref,
    table,
    stage,
    keys,
    values,
    keys_t,
    q_ref,
    g_ref,
    dq_ref,
    score,
    dprob,
    expo,
    sgrad,
    acc,
    cacc_k,
    cacc_v,
    in_sems,
    out_sems,
):
    chips = cand_count // 2
    own_rows = own_ref.shape[1]
    windows = per_device
    steps = heads * windows
    prompt_len = keys.shape[1]
    half = prompt_len // 2
    levels = 3 if half % (3 * 128) == 0 else 1
    chunk = math.gcd(half, 128)
    band = 2 * window
    lanes = group * window
    head_columns = q_ref.shape[2]
    groups = head_columns // HEAD_WIDTH // group
    scale = 1.0 / math.sqrt(HEAD_WIDTH)
    factor = scale * math.log2(math.e)
    width = heads * HEAD_WIDTH
    my_cand = where_ref[0]
    my_core = lax.rem(my_cand, 2)

    def copy_in(t, which):
        src, dst = ((q_hbm, q_ref), (g_hbm, g_ref))[which]
        h, w = divmod(t, windows)
        return pltpu.make_async_copy(
            src.at[w * window : (w + 1) * window, h * head_columns : (h + 1) * head_columns],
            dst.at[t],
            in_sems.at[which, t],
        )

    def copy_out(t):
        h, w = divmod(t, windows)
        return pltpu.make_async_copy(
            dq_ref.at[t],
            dq_hbm.at[w * window : (w + 1) * window, h * head_columns : (h + 1) * head_columns],
            out_sems.at[t],
        )

    for t in range(steps):
        copy_in(t, 0).start()
        copy_in(t, 1).start()

    def visit(k, carry):
        count, place = carry
        mine = assign_ref[k] == my_cand

        @pl.when(mine)
        def _():
            table[0, count] = place
            table[1, count] = place + lengths_ref[k]
            table[2, count] = offsets_ref[k]

        return (
            count + mine.astype(jnp.int32),
            place + jnp.where(mine, lengths_ref[k], 0),
        )

    lax.fori_loop(0, assign_ref.shape[0], visit, (jnp.int32(0), jnp.int32(0)))
    filled = table[1, per_device - 1]

    def token_base(q, z, core):
        return pl.multiple_of((q * cand_count + 2 * z + core) * own_rows, 8)

    for ref, core in ((own_ref, my_core), (other_ref, 1 - my_core)):
        for q in range(prefix_count):
            for z in range(chips):
                stage[pl.ds(token_base(q, z, core), own_rows), :] = ref[q * chips + z].astype(F32)
    for h in range(heads):
        k_block = stage[:, h * HEAD_WIDTH : (h + 1) * HEAD_WIDTH]
        keys[h] = k_block.astype(BF16)
        keys_t[h] = k_block.T.astype(BF16)
        values[h] = stage[:, width + h * HEAD_WIDTH : width + (h + 1) * HEAD_WIDTH].astype(BF16)
    acc[...] = jnp.zeros_like(acc)
    cacc_k[...] = jnp.zeros_like(cacc_k)
    cacc_v[...] = jnp.zeros_like(cacc_v)

    def fold(x, op):
        return op(x.reshape(x.shape[0] // 8, 8, x.shape[1]), axis=0)

    def attend(t, prompt_rows):
        head = t // windows
        first_row = lax.rem(t, windows) * window
        band_row = pl.multiple_of(jnp.maximum(first_row - window, 0), window)
        row = first_row + lax.broadcasted_iota(jnp.int32, (1, lanes), 1) % window
        offset = jnp.zeros((1, lanes), jnp.int32)
        start = jnp.full((1, lanes), windows * window, jnp.int32)
        for c in range(per_device):
            inside = (row >= table[0, c]) & (row < table[1, c])
            offset = jnp.where(inside, table[2, c], offset)
            start = jnp.where(inside, table[0, c], start)
        valid = row < filled
        blocks = [(i * chunk, chunk) for i in range(prompt_rows // chunk)]
        every = blocks + [(prompt_len, band)]
        cont_place = band_row + lax.broadcasted_iota(jnp.int32, (band, lanes), 0)
        cont_seen = (cont_place >= start) & (cont_place <= row)
        ck = ck_ref[head, pl.ds(band_row, band), :]
        cv = cv_ref[head, pl.ds(band_row, band), :]

        def rows_of(ref, index):
            return jnp.concatenate(
                [
                    ref[t, :, (index * group + h) * HEAD_WIDTH : (index * group + h + 1) * HEAD_WIDTH]
                    for h in range(group)
                ],
                axis=0,
            )

        qs = [rows_of(q_ref, i) for i in range(groups)]
        gs = [rows_of(g_ref, i) for i in range(groups)]
        cols = [slice(i * lanes, (i + 1) * lanes) for i in range(groups)]
        tops = []
        for i in range(groups):
            top = jnp.full((8, lanes), MASKED_SCORE, F32)
            for first, size in every:
                k = keys[head, first : first + size] if first < prompt_len else ck
                s = lax.dot_general(k, qs[i], DIMS_NT, preferred_element_type=F32) * factor
                if first == prompt_len:
                    s = jnp.where(cont_seen, s, MASKED_SCORE)
                elif first >= half:
                    place = first + lax.broadcasted_iota(jnp.int32, s.shape, 0)
                    s = jnp.where(place < offset, s, MASKED_SCORE)
                score[first : first + size, cols[i]] = s
                top = jnp.maximum(top, fold(s, jnp.max))
            tops.append(jnp.max(top, axis=0, keepdims=True))
        totals, deltas = [], []
        for i in range(groups):
            total = jnp.zeros((8, lanes), F32)
            delta = jnp.zeros((8, lanes), F32)
            for first, size in every:
                v = values[head, first : first + size] if first < prompt_len else cv
                dp = lax.dot_general(v, gs[i], DIMS_NT, preferred_element_type=F32)
                e = jnp.exp2(score[first : first + size, cols[i]] - tops[i])
                dprob[first : first + size, cols[i]] = dp
                expo[first : first + size, cols[i]] = e.astype(BF16)
                total = total + fold(e, jnp.sum)
                delta = delta + fold(e * dp, jnp.sum)
            totals.append(jnp.sum(total, axis=0, keepdims=True))
            deltas.append(jnp.sum(delta, axis=0, keepdims=True))
        inverses, scaled_q, scaled_g = [], [], []
        for i in range(groups):
            inverse = jnp.where(valid, 1.0 / totals[i], 0.0)
            delta = deltas[i] / totals[i]
            for first, size in every:
                e = expo[first : first + size, cols[i]].astype(F32)
                sgrad[first : first + size, cols[i]] = (
                    e * (dprob[first : first + size, cols[i]] - delta)
                ).astype(BF16)
            column = jnp.broadcast_to(inverse, (HEAD_WIDTH, lanes)).T
            scaled_q.append((qs[i].astype(F32) * (column * scale)).astype(BF16))
            scaled_g.append((gs[i].astype(F32) * column).astype(BF16))
            inverses.append(inverse)
        g_all = jnp.concatenate(scaled_g, axis=0)
        q_all = jnp.concatenate(scaled_q, axis=0)
        acc[head, :prompt_rows, HEAD_WIDTH:] += lax.dot_general(
            expo[:prompt_rows, :], g_all, DIMS_NN, preferred_element_type=F32
        )
        cacc_v[head, pl.ds(band_row, band), :] += lax.dot_general(
            expo[prompt_len:, :], g_all, DIMS_NN, preferred_element_type=F32
        )
        acc[head, :prompt_rows, :HEAD_WIDTH] += lax.dot_general(
            sgrad[:prompt_rows, :], q_all, DIMS_NN, preferred_element_type=F32
        )
        cacc_k[head, pl.ds(band_row, band), :] += lax.dot_general(
            sgrad[prompt_len:, :], q_all, DIMS_NN, preferred_element_type=F32
        )
        ck_t = ck.astype(F32).T.astype(BF16)
        for i in range(groups):
            dq_t = lax.dot_general(
                keys_t[head, :, :prompt_rows],
                sgrad[:prompt_rows, cols[i]],
                DIMS_NN,
                preferred_element_type=F32,
            ) + lax.dot_general(
                ck_t, sgrad[prompt_len:, cols[i]], DIMS_NN, preferred_element_type=F32
            )
            dq = (dq_t * (inverses[i] * scale)).T.astype(BF16)
            for h in range(group):
                place = (i * group + h) * HEAD_WIDTH
                dq_ref[t, :, place : place + HEAD_WIDTH] = dq[h * window : (h + 1) * window]

    for t in range(steps):
        copy_in(t, 0).wait()
        copy_in(t, 1).wait()

    def step(t, carry):
        first_row = lax.rem(t, windows) * window
        reach = jnp.int32(0)
        for c in range(per_device):
            meets = (table[0, c] < first_row + window) & (table[1, c] > first_row)
            reach = jnp.maximum(reach, jnp.where(meets, table[2, c], 0))
        grain = half // levels
        level = jnp.where(
            first_row >= filled, levels + 1, (jnp.maximum(reach - half, 0) + grain - 1) // grain
        )
        for n in range(levels + 1):

            @pl.when(level == n)
            def _(n=n):
                attend(t, half + n * grain)

        @pl.when(level == levels + 1)
        def _():
            dq_ref[t] = jnp.zeros(dq_ref.shape[1:], BF16)

        return carry

    lax.fori_loop(0, steps, step, jnp.int32(0))
    for t in range(steps):
        copy_out(t).start()
    for h in range(heads):
        here = slice(h * HEAD_WIDTH, (h + 1) * HEAD_WIDTH)
        dck_ref[:, here] = cacc_k[h].astype(BF16)
        dcv_ref[:, here] = cacc_v[h].astype(BF16)
    for ref, core in ((keep_ref, my_core), (send_ref, 1 - my_core)):
        for q in range(prefix_count):
            for z in range(chips):
                for h in range(heads):
                    block = acc[h, pl.ds(token_base(q, z, core), own_rows), :].astype(BF16)
                    here = slice(h * HEAD_WIDTH, (h + 1) * HEAD_WIDTH)
                    ref[q * chips + z, :, here] = block[:, :HEAD_WIDTH]
                    there = slice(width + h * HEAD_WIDTH, width + (h + 1) * HEAD_WIDTH)
                    ref[q * chips + z, :, there] = block[:, HEAD_WIDTH:]
    for t in range(steps):
        copy_out(t).wait()


def attention(
    where, assign, lengths, offsets, own, other, query, grad_out, cont_key, cont_value, axes
):
    prefix_count, cand_count = axes
    rows, query_width = query.shape
    heads = cont_key.shape[1] // HEAD_WIDTH
    head_columns = query_width // heads
    per_device = assign.shape[0] // cand_count
    window = rows // per_device
    piece_width = own.shape[2]
    prompt_len = 2 * own.shape[0] * own.shape[1]
    group = min(max(256 // window, 1), head_columns // HEAD_WIDTH)
    all_lanes = head_columns // HEAD_WIDTH * window
    joined = prompt_len + 2 * window
    steps = heads * per_device
    in_hbm = pl.BlockSpec(memory_space=pl.ANY)

    def by_head(x):
        return jnp.stack([x[:, h * HEAD_WIDTH : (h + 1) * HEAD_WIDTH] for h in range(heads)])

    return pl.pallas_call(
        functools.partial(
            attention_body, prefix_count, cand_count, window, per_device, heads, group
        ),
        in_specs=[smem_spec()] * 4 + [vmem_spec()] * 4 + [in_hbm] * 2,
        out_specs=[in_hbm] + [vmem_spec()] * 4,
        scratch_shapes=[
            pltpu.SMEM((3, per_device), jnp.int32),
            pltpu.VMEM((prompt_len, piece_width), F32),
            pltpu.VMEM((heads, prompt_len, HEAD_WIDTH), BF16),
            pltpu.VMEM((heads, prompt_len, HEAD_WIDTH), BF16),
            pltpu.VMEM((heads, HEAD_WIDTH, prompt_len), BF16),
            pltpu.VMEM((steps, window, head_columns), BF16),
            pltpu.VMEM((steps, window, head_columns), BF16),
            pltpu.VMEM((steps, window, head_columns), BF16),
            pltpu.VMEM((joined, all_lanes), F32),
            pltpu.VMEM((joined, all_lanes), F32),
            pltpu.VMEM((joined, all_lanes), BF16),
            pltpu.VMEM((joined, all_lanes), BF16),
            pltpu.VMEM((heads, prompt_len, 2 * HEAD_WIDTH), F32),
            pltpu.VMEM((heads, rows, HEAD_WIDTH), F32),
            pltpu.VMEM((heads, rows, HEAD_WIDTH), F32),
            pltpu.SemaphoreType.DMA((2, steps)),
            pltpu.SemaphoreType.DMA((steps,)),
        ],
        out_shape=[
            jax.ShapeDtypeStruct(query.shape, BF16),
            jax.ShapeDtypeStruct(cont_key.shape, BF16),
            jax.ShapeDtypeStruct(cont_value.shape, BF16),
            jax.ShapeDtypeStruct(own.shape, BF16),
            jax.ShapeDtypeStruct(own.shape, BF16),
        ],
        compiler_params=pltpu.CompilerParams(vmem_limit_bytes=VMEM_BYTES),
        cost_estimate=pl.CostEstimate(
            flops=10 * query.size * joined,
            bytes_accessed=8 * query.size,
            transcendentals=query.size * 4,
        ),
        name="attention_backward",
    )(
        where,
        assign,
        lengths,
        offsets,
        own,
        other,
        by_head(cont_key),
        by_head(cont_value),
        query,
        grad_out,
    )


def per_device(
    query,
    grad_out,
    continuation_key,
    continuation_value,
    prompt_key,
    shared_prompt_value,
    assign,
    lengths,
    offsets,
):
    prefix_count = lax.axis_size("prefix")
    cand_count = lax.axis_size("cand")
    chips = cand_count // 2
    where = jnp.reshape(lax.axis_index("cand"), (1,)).astype(jnp.int32)
    same_core = [
        [p * cand_count + 2 * z + core for p in range(prefix_count) for z in range(chips)]
        for core in range(2)
    ]

    def exchange(x):
        return lax.all_to_all(
            x, ("prefix", "cand"), 0, 0, tiled=True, axis_index_groups=same_core
        )

    def to_sibling(x):
        return lax.ppermute(x, "cand", [(i, i ^ 1) for i in range(cand_count)])

    own = exchange(split_heads(prompt_key, shared_prompt_value, prefix_count, chips))
    query_grad, cont_key_grad, cont_value_grad, kept, sent = attention(
        where,
        assign,
        lengths,
        offsets,
        own,
        to_sibling(own),
        query,
        grad_out,
        continuation_key,
        continuation_value,
        (prefix_count, cand_count),
    )
    by_chip = exchange(add_sibling(kept, to_sibling(sent)))
    prompt_key_grad, prompt_value_grad = add_chips(by_chip, prefix_count, chips)
    return (query_grad, cont_key_grad, cont_value_grad, prompt_key_grad, prompt_value_grad)


def solution(mesh):
    in_specs = (
        P("cand", "prefix"),
        P("cand", "prefix"),
        P("cand", "prefix"),
        P("cand", "prefix"),
        P(("prefix", "cand"), None),
        P(("prefix", "cand"), None),
        P(),
        P(),
        P(),
    )
    out_specs = (
        P("cand", "prefix"),
        P("cand", "prefix"),
        P("cand", "prefix"),
        P(("prefix", "cand"), None),
        P(("prefix", "cand"), None),
    )
    return jax.shard_map(
        per_device, mesh=mesh, in_specs=in_specs, out_specs=out_specs, check_vma=False
    )
```

time: 67.2 us -> 64.4 us (0.958); the launches traced: 66.9 us -> 64.8 us
  blocking collectives: 0 us -> 41.2 us
  starting transfers between devices: 25.7 us -> 4.3 us
  waiting for transfers between devices: 21.8 us -> 2.13 us
  Pallas kernels: 14.5 us -> 13.3 us
  local copies, waits for them, and re-layouts: 4.06 us -> 3.17 us
    all_to_all x0 -> x2, blocking collectives: none -> 41.2 us  [exchange(): lax.all_to_all(x, ('prefix', 'cand'), 0, 0, tiled=True, axis_index_groups...]
    ppermute x12 -> x0, waiting for transfers between devices: 19.5 us -> none  [the longest x6 13.8 us: along_chips(): lax.ppermute(x, 'cand', [(i, (i + 2 * step) % cand_count) for i in range(...]
    ppermute x12 -> x0, starting transfers between devices: 17.7 us -> none  [the longest x6 9.13 us: along_prefix(): lax.ppermute(x, 'prefix', [(i, (i + step) % prefix_count) for i in range(...]
    ppermute x5 -> x2, starting transfers between devices: 8.05 us -> 4.3 us  [to_sibling(): return lax.ppermute(x, 'cand', [(i, i ^ 1) for i in range(cand_count)])]
    unnamed x18 -> x16, local copies, waits for them, and re-layouts: 4.06 us -> 2.27 us
    pallas_call x5 -> x2, Pallas kernels: 1.91 us -> 0.77 us  [glue_call(): pl.pallas_call(body, out_shape=out_shape, in_specs=[smem_spec()] * scalar...]
    another operation x0 -> x2, local copies, waits for them, and re-layouts: none -> 0.89 us  [by_head(): jnp.stack([x[:, h * HEAD_WIDTH:(h + 1) * HEAD_WIDTH] for h in range(heads)])]
    ppermute x5 -> x2, waiting for transfers between devices: 2.29 us -> 2.13 us  [to_sibling(): return lax.ppermute(x, 'cand', [(i, i ^ 1) for i in range(cand_count)])]
  transfers between devices with their start and end apart: 17 -> 2, of which waited for: 12 -> 2; matrix products, arithmetic and copies ran while one was open for 0% -> 1% of each run, Pallas kernels for 0% -> 0%
where the time goes in v2:
time: 64.4 us; the launch traced here: 64.8 us
  blocking collectives  41.2 us (64%)
  Pallas kernels  13.3 us (21%)
  starting transfers between devices  4.3 us (7%)
  local copies, waits for them, and re-layouts  3.17 us (5%)
  waiting for transfers between devices  2.13 us (3%)
  between operations  0.71 us (1%)
    all_to_all x2, blocking collectives, exchange(): lax.all_to_all(x, ('prefix', 'cand'), 0, 0, tiled=True, axis_index_groups...  41.2 us
    pallas_call x1, Pallas kernels, attention(): pl.pallas_call(functools.partial(attention_body, prefix_count, cand_count...  12.4 us
    ppermute x2, starting transfers between devices, to_sibling(): return lax.ppermute(x, 'cand', [(i, i ^ 1) for i in range(cand_count)])  4.3 us
    unnamed x16, local copies, waits for them, and re-layouts  2.27 us
    ppermute x2, waiting for transfers between devices, to_sibling(): return lax.ppermute(x, 'cand', [(i, i ^ 1) for i in range(cand_count)])  2.13 us
  transfers between devices with their start and end apart: 2, of which 2 were waited for; matrix products, arithmetic and copies ran while one was open for 1% of the time, Pallas kernels for 0%

profile of v2, /device:TPU:0, one launch (start us, length us, event | category | flops | bytes accessed | tf_op | source)
XLA Modules:
  0.0 64.8 jit_solution(16889144094200362494)
XLA Ops:
  0.6 0.0 copy-start
  0.6 0.8 %copy-done = bf16[24,1024]{1,0:T(8,128)(2,1)S(1)} copy-done((bf16[24,1024]{1,0:T(8,128)(2,1)S(1)}, bf16[24,1024]{1,0:T(8,128)(2,1)}, u32[]{:S(2)}) %copy-start) | copy-done | bytes 49176
  1.4 0.0 copy-start.1
  1.4 0.8 %copy-done.1 = bf16[24,1024]{1,0:T(8,128)(2,1)S(1)} copy-done((bf16[24,1024]{1,0:T(8,128)(2,1)S(1)}, bf16[24,1024]{1,0:T(8,128)(2,1)}, u32[]{:S(2)}) %copy-start.1) | copy-done | bytes 49176
  2.2 0.0 copy-start.7
  2.2 0.0 copy-start.3
  2.2 0.2 split_heads.1
  2.4 0.0 copy-start.2
  2.4 21.6 %all_to_all.10.own_ref = bf16[16,24,512]{2,1,0:T(8,128)(2,1)S(1)} all-to-all(bf16[16,24,512]{2,1,0:T(8,128)(2,1)S(1)} %split_heads.1), channel_id=1, replica_groups={{0,2,4,6,8,10,12,14,16,18,20,22,24,26,28,30},{1,3,5,7,9,11,13,15,17,19,..., dimensions={0} | all-to-all | bytes 786432 | tf_op jit(solution)/shard_map/all_to_all | solution.py:456
  24.0 0.0 collective-permute-start
  24.0 0.0 copy-done.7
  24.1 0.9 %slice_bitcast_fusion.1 = (bf16[1,256,128]{2,1,0:T(8,128)(2,1)S(1)}, bf16[1,256,128]{2,1,0:T(8,128)(2,1)S(1)}) fusion(bf16[256,256]{1,0:T(8,128)(2,1)} %param.12), kind=kLoop, calls=%fused_computation.3 | loop fusion | bytes 262144 | tf_op jit(solution)/shard_map/stack | solution.py:380
  25.0 0.8 %collective-permute-done.other_ref = bf16[16,24,512]{2,1,0:T(8,128)(2,1)S(1)} collective-permute-done((bf16[16,24,512]{2,1,0:T(8,128)(2,1)S(1)}, bf16[16,24,512]{2,1,0:T(8,128)(2,1)S(1)}, u32[]{:S(2)}, u32[]{:S(2)}) %collective-permute-start) | collective-permute-done | bytes 393248 | tf_op jit(solution)/shard_map/ppermute | solution.py:461
  25.8 0.0 copy-start.4
  25.8 0.0 copy-start.5
  25.8 0.0 copy-start.6
  25.8 0.0 copy-done.3
  25.8 0.0 copy-done.2
  25.8 0.6 copy-done.4
  26.4 0.0 copy-done.5
  26.4 0.0 copy-done.6
  26.4 12.4 %attention_backward.1 = (bf16[256,2048]{1,0:T(8,128)(2,1)}, bf16[256,256]{1,0:T(8,128)(2,1)}, bf16[256,256]{1,0:T(8,128)(2,1)}, bf16[16,24,512]{2,1,0:T(8,128)(2,1)S(1)}, bf16[16,24,512]{2,1,0:T(8,128)(2,1)S(1)}) custom-call(s32[1]{0:T(128)} %bitcast.where_ref, s32[32]{0:T(128)S(1)} %copy-done.4, s32[32]{0:T(128)S(1)} %copy-done.5, s32[32]{0:T(128)S(1)} %copy-done.6, ...), custom_call_target="tpu_custom_call" | custom-call | flops 4697620480 | bytes 4194304 | tf_op jit(solution)/shard_map/attention_backward/pallas_call | solution.py:382
  38.8 4.3 %collective-permute-start.1 = (bf16[16,24,512]{2,1,0:T(8,128)(2,1)S(1)}, bf16[16,24,512]{2,1,0:T(8,128)(2,1)S(1)}, u32[]{:S(2)}, u32[]{:S(2)}) collective-permute-start(bf16[16,24,512]{2,1,0:T(8,128)(2,1)S(1)} %get-tuple-element.16), channel_id=1, source_target_pairs={{0,1},{1,0},{2,3},{3,2},{4,5},{5,4},{6,7},{7,6},{8,9},{9,8},{10,11... | collective-permute-start | bytes 1179656 | tf_op jit(solution)/shard_map/ppermute | solution.py:461
  43.1 1.3 %collective-permute-done.1.arrived_ref = bf16[16,24,512]{2,1,0:T(8,128)(2,1)S(1)} collective-permute-done((bf16[16,24,512]{2,1,0:T(8,128)(2,1)S(1)}, bf16[16,24,512]{2,1,0:T(8,128)(2,1)S(1)}, u32[]{:S(2)}, u32[]{:S(2)}) %collective-permute-start.1) | collective-permute-done | bytes 393248 | tf_op jit(solution)/shard_map/ppermute | solution.py:461
  44.5 0.1 add_sibling.1
  44.6 19.6 %all_to_all.11.piece_ref = bf16[16,24,512]{2,1,0:T(8,128)(2,1)S(1)} all-to-all(bf16[16,24,512]{2,1,0:T(8,128)(2,1)S(1)} %add_sibling.1), channel_id=1, replica_groups={{0,2,4,6,8,10,12,14,16,18,20,22,24,26,28,30},{1,3,5,7,9,11,13,15,17,19,..., dimensions={0} | all-to-all | bytes 786432 | tf_op jit(solution)/shard_map/all_to_all | solution.py:456
  64.2 0.7 %add_chips.1 = (bf16[24,1024]{1,0:T(8,128)(2,1)}, bf16[24,1024]{1,0:T(8,128)(2,1)}) custom-call(bf16[16,24,512]{2,1,0:T(8,128)(2,1)S(1)} %all_to_all.11.piece_ref), custom_call_target="tpu_custom_call" | custom-call | tf_op jit(solution)/shard_map/add_chips/pallas_call | solution.py:30
  (2 shorter events, 0.0 us)
Async XLA Ops:
  0.6 0.8 %copy-start = (bf16[24,1024]{1,0:T(8,128)(2,1)S(1)}, bf16[24,1024]{1,0:T(8,128)(2,1)}, u32[]{:S(2)}) copy-start(bf16[24,1024]{1,0:T(8,128)(2,1)} %key_hbm.1) | copy-start | bytes 147460
  1.4 0.8 %copy-start.1 = (bf16[24,1024]{1,0:T(8,128)(2,1)S(1)}, bf16[24,1024]{1,0:T(8,128)(2,1)}, u32[]{:S(2)}) copy-start(bf16[24,1024]{1,0:T(8,128)(2,1)} %value_hbm.1) | copy-start | bytes 147460
  2.2 21.8 %copy-start.7 = (bf16[256,256]{1,0:T(8,128)(2,1)S(1)}, bf16[256,256]{1,0:T(8,128)(2,1)}, u32[]{:S(2)}) copy-start(bf16[256,256]{1,0:T(8,128)(2,1)} %param.11) | copy-start | bytes 393220
  2.2 23.5 %copy-start.3 = (bf16[256,2048]{1,0:T(8,128)(2,1)S(1)}, bf16[256,2048]{1,0:T(8,128)(2,1)}, u32[]{:S(2)}) copy-start(bf16[256,2048]{1,0:T(8,128)(2,1)} %g_hbm.1) | copy-start | bytes 3145732
  2.4 23.4 %copy-start.2 = (bf16[256,2048]{1,0:T(8,128)(2,1)S(1)}, bf16[256,2048]{1,0:T(8,128)(2,1)}, u32[]{:S(2)}) copy-start(bf16[256,2048]{1,0:T(8,128)(2,1)} %q_hbm.1) | copy-start | bytes 3145732
  24.0 1.7 %collective-permute-start = (bf16[16,24,512]{2,1,0:T(8,128)(2,1)S(1)}, bf16[16,24,512]{2,1,0:T(8,128)(2,1)S(1)}, u32[]{:S(2)}, u32[]{:S(2)}) collective-permute-start(bf16[16,24,512]{2,1,0:T(8,128)(2,1)S(1)} %all_to_all.10.own_ref), channel_id=1, source_target_pairs={{0,1},{1,0},{2,3},{3,2},{4,5},{5,4},{6,7},{7,6},{8,9},{9,8},{10,11... | collective-permute-start | bytes 1179656 | tf_op jit(solution)/shard_map/ppermute | solution.py:461
  25.8 0.7 %copy-start.4 = (s32[32]{0:T(128)S(1)}, s32[32]{0:T(128)}, u32[]{:S(2)}) copy-start(s32[32]{0:T(128)} %assign_ref.1) | copy-start | bytes 388
  25.8 0.7 %copy-start.5 = (s32[32]{0:T(128)S(1)}, s32[32]{0:T(128)}, u32[]{:S(2)}) copy-start(s32[32]{0:T(128)} %lengths_ref.1) | copy-start | bytes 388
  25.8 0.7 %copy-start.6 = (s32[32]{0:T(128)S(1)}, s32[32]{0:T(128)}, u32[]{:S(2)}) copy-start(s32[32]{0:T(128)} %offsets_ref.1) | copy-start | bytes 388
  38.8 5.6 %collective-permute-start.1 = (bf16[16,24,512]{2,1,0:T(8,128)(2,1)S(1)}, bf16[16,24,512]{2,1,0:T(8,128)(2,1)S(1)}, u32[]{:S(2)}, u32[]{:S(2)}) collective-permute-start(bf16[16,24,512]{2,1,0:T(8,128)(2,1)S(1)} %get-tuple-element.16), channel_id=1, source_target_pairs={{0,1},{1,0},{2,3},{3,2},{4,5},{5,4},{6,7},{7,6},{8,9},{9,8},{10,11... | collective-permute-start | bytes 1179656 | tf_op jit(solution)/shard_map/ppermute | solution.py:461
